TPU v7x, 32 devices: a whole 2x2x4 slice. The times are simulated.
32 devices in a mesh: seq: 4 (over y, x), table: 8 (over z, core).
Axes of the slice: x: 2, y: 2, z: 4, core: 2. Of those that a mesh axis runs over, the one named last changes fastest.
Arguments:
- events_x: bfloat16 [8, 512, 512], P('table', 'seq'), may hold values from -6 to 6
- proj: bfloat16 [512, 1536], replicated, may hold values from -0.25 to 0.25
- out_grad: bfloat16 [8, 512, 512], P('table', 'seq'), may hold values from -6 to 6
- block_mask: int32 [4, 4], replicated, may hold values 0 or 1
- item_ids: int32 [8, 512], P('table', 'seq'), may hold values from 0 to 4095, as said below
- owner_of: int32 [4096], replicated, may hold values from 0 to 7, as said below
- local_of: int32 [4096], replicated, may hold values from 0 to 511, as said below
- table: bfloat16 [4096, 512], P('table'), may hold values from -3 to 3
- moment: float32 [4096, 512], P('table'), may hold values from -2 to 2
- second: float32 [4096], P('table'), may hold values from 0.05 to 2
Outputs:
- new_table: bfloat16 [4096, 512], P('table')
- new_moment: float32 [4096, 512], P('table')
- new_second: float32 [4096], P('table')
- event_rows: bfloat16 [8, 512, 512], P('table', 'seq')
Inputs may be any that keep to these rules, and one draw needn't show every extreme that they name: `item_ids`: among the 128 events of one device (one history, one seq index), at most 32 have items of one owner (owner_of); in every draw, for each seq index, some owner gets exactly 32 from the device of every history. owner_of[r] * 512 + local_of[r] takes every value of 0 to 4095 once over the items r. `local_of`: see owner_of.
All inputs are finite; a program needn't handle non-finite values.
Results may differ from a plain program's by a relative error of at most 0.0075.
Values may be sent and summed in bfloat16 or wider, within the bound.
A program may use at most 64 MiB of HBM per device.

v0:
```python
import math

import jax
import jax.numpy as jnp
from jax import lax
from jax.sharding import PartitionSpec as P

HEADS = 8


first_decay = 0.9
second_decay = 0.99
step_rate = 0.05
epsilon = 1e-08


def block_length(piece_rows):
    block_rows = piece_rows
    while block_rows > 1024 and block_rows % 2 == 0:
        block_rows = block_rows // 2
    return block_rows


def adam_update(item_grad, moment, second, table):
    new_moment = first_decay * moment + (1.0 - first_decay) * item_grad
    new_second = second_decay * second + (1.0 - second_decay) * jnp.mean(
        item_grad * item_grad, axis=1
    )
    new_table = (
        table.astype(jnp.float32)
        - step_rate * new_moment / (jnp.sqrt(new_second) + epsilon)[:, None]
    ).astype(jnp.bfloat16)
    return (new_table, new_moment, new_second)


def body(events_x, proj, out_grad, block_mask, item_ids, owner_of, local_of, table, moment, second):
    tokens = events_x.shape[1]
    features = events_x.shape[2]
    head_size = features // HEADS
    seq_count = lax.axis_size("seq")
    owner_count = lax.axis_size("table")
    position = lax.axis_index("seq")
    history_scale = 1.0 / math.sqrt(tokens * seq_count)
    temper = 1.0 / math.sqrt(head_size)
    block_ids = jnp.arange(seq_count)
    inputs = events_x[0]
    cotangent = out_grad[0]
    projected = jnp.dot(inputs, proj, preferred_element_type=jnp.float32).astype(jnp.bfloat16)
    queries = projected[:, :features]
    key_mat = projected[:, features : 2 * features]
    value_mat = projected[:, 2 * features :]
    own_pos = position * tokens + jnp.arange(tokens)
    visible_col = lax.dynamic_slice_in_dim(block_mask, position, 1, 1)[:, 0]

    def split_heads(matrix):
        return matrix.reshape(matrix.shape[0], HEADS, head_size)

    def pair_terms(query_block, grad_block, key_block, value_block, allowed):
        scores = (
            jnp.einsum(
                "qhe,khe->hqk",
                split_heads(query_block),
                split_heads(key_block),
                preferred_element_type=jnp.float32,
            )
            * temper
        )
        gates = jax.nn.sigmoid(scores)
        weights = (scores * gates * history_scale * allowed).astype(jnp.bfloat16)
        slopes = gates * (1.0 + scores * (1.0 - gates))
        attn_grad = jnp.einsum(
            "qhe,khe->hqk",
            split_heads(grad_block),
            split_heads(value_block),
            preferred_element_type=jnp.float32,
        )
        score_grad = (attn_grad * slopes * (history_scale * temper) * allowed).astype(jnp.bfloat16)
        return (weights, score_grad)

    zero_rows = jnp.zeros((tokens, features), jnp.float32)
    zero_terms = jnp.zeros((tokens * seq_count, features), jnp.float32)
    query_piece = lax.all_gather(queries, "seq", axis=0, tiled=True)
    grad_piece = lax.all_gather(cotangent, "seq", axis=0, tiled=True)
    block_rows = block_length(query_piece.shape[0])

    def advance(block_index, running):
        first_row = block_index * block_rows
        query_block = lax.dynamic_slice_in_dim(query_piece, first_row, block_rows, 0)
        grad_block = lax.dynamic_slice_in_dim(grad_piece, first_row, block_rows, 0)
        query_pos = first_row + jnp.arange(block_rows)
        query_blk = query_pos // tokens
        visible = jnp.any(
            (query_blk[:, None] == block_ids[None, :]) & (visible_col[None, :] == 1), axis=1
        ) | (query_blk == position)
        allowed = (visible[:, None] & (own_pos[None, :] <= query_pos[:, None])).astype(jnp.float32)

        def accumulate(current):
            weights, score_grad = pair_terms(query_block, grad_block, key_mat, value_mat, allowed)
            value_total = current[1] + jnp.einsum(
                "hqk,qhe->khe", weights, split_heads(grad_block), preferred_element_type=jnp.float32
            ).reshape(tokens, features)
            key_total = current[0] + jnp.einsum(
                "hqk,qhe->khe",
                score_grad,
                split_heads(query_block),
                preferred_element_type=jnp.float32,
            ).reshape(tokens, features)
            query_part = jnp.einsum(
                "hqk,khe->qhe", score_grad, split_heads(key_mat), preferred_element_type=jnp.float32
            ).reshape(block_rows, features)
            query_terms = lax.dynamic_update_slice(
                current[2], query_part, (first_row, jnp.int32(0))
            )
            return (key_total, value_total, query_terms)

        return lax.cond(jnp.any(allowed > 0), accumulate, lambda current: current, running)

    key_grad, value_grad, query_terms = lax.fori_loop(
        0, query_piece.shape[0] // block_rows, advance, (zero_rows, zero_rows, zero_terms)
    )
    query_grad = lax.psum_scatter(query_terms, "seq", scatter_dimension=0, tiled=True)
    stacked = jnp.concatenate([query_grad, key_grad, value_grad], axis=1).astype(jnp.bfloat16)
    input_grad = lax.dot_general(
        stacked, proj, (((1,), (1,)), ((), ())), preferred_element_type=jnp.float32
    ).astype(jnp.bfloat16)
    event_items = item_ids[0]
    owners = owner_of[event_items]
    slab_index = local_of[event_items]
    capacity = 2 * tokens // owner_count
    owner_hits = (owners[:, None] == jnp.arange(owner_count)[None, :]).astype(jnp.int32)
    slots = jnp.sum(jnp.cumsum(owner_hits, axis=0) * owner_hits, axis=1) - 1
    target = owners * capacity + slots
    send_rows = (
        jnp.zeros((owner_count * capacity, features), jnp.bfloat16)
        .at[target]
        .set(input_grad)
        .reshape(owner_count, capacity, features)
    )
    send_index = (
        jnp.full((owner_count * capacity,), -1, jnp.int32)
        .at[target]
        .set(slab_index)
        .reshape(owner_count, capacity)
    )
    got_rows, got_index = (
        lax.all_to_all(send_rows, "table", split_axis=0, concat_axis=0, tiled=True),
        lax.all_to_all(send_index, "table", split_axis=0, concat_axis=0, tiled=True),
    )
    slab_rows = table.shape[0]
    select = (got_index.reshape(-1)[None, :] == jnp.arange(slab_rows)[:, None]).astype(jnp.bfloat16)
    slab_grad = jnp.dot(select, got_rows.reshape(-1, features), preferred_element_type=jnp.float32)
    item_grad = lax.psum(slab_grad.astype(jnp.bfloat16), "seq").astype(jnp.float32)
    new_table, new_moment, new_second = adam_update(item_grad, moment, second, table)
    clamped = jnp.clip(got_index, 0, slab_rows - 1)
    replies = jnp.where(
        (got_index >= 0)[:, :, None], new_table[clamped], jnp.zeros((), jnp.bfloat16)
    )
    returned_rows = lax.all_to_all(replies, "table", split_axis=0, concat_axis=0, tiled=True)
    event_rows = returned_rows.reshape(owner_count * capacity, features)[target]
    return (new_table, new_moment, new_second, event_rows[None])


def solution(mesh):
    return jax.shard_map(
        body,
        mesh=mesh,
        in_specs=(
            P("table", "seq", None),
            P(),
            P("table", "seq", None),
            P(),
            P("table", "seq"),
            P(),
            P(),
            P("table", None),
            P("table", None),
            P("table"),
        ),
        out_specs=(P("table", None), P("table", None), P("table"), P("table", "seq", None)),
        check_vma=False,
    )
```

profile of v0, /device:TPU:0, one launch (start us, length us, event | category | flops | bytes accessed | tf_op | source)
XLA Modules:
  0.0 160.5 jit_solution(8339865922844851063)
XLA Ops:
  7.2 0.0 copy-start
  7.2 0.0 reduce-scatter.2.cloned.1.call-start
  7.3 1.0 fusion.22
  8.2 0.1 fusion.18
  8.3 0.2 copy-done
  8.6 1.3 convolution_convert_fusion
  9.9 11.5 %all_gather.7 = bf16[512,512]{1,0:T(8,128)(2,1)S(1)} all-gather(bf16[128,512]{1,0:T(8,128)(2,1)S(1)} %slice.22), channel_id=1, replica_groups=mesh['seq'=4,'table'=8] {'seq'}, dimensions={0}, use_global_device_ids=true | all-gather | bytes 655360 | tf_op jit(solution)/shard_map/all_gather | solution.py:82
  21.4 0.1 copy.28
  21.5 11.3 %all-gather = bf16[1,512,512]{1,2,0:T(8,128)(2,1)} all-gather(bf16[1,128,512]{1,2,0:T(8,128)(2,1)S(1)} %copy.28), channel_id=2, replica_groups=mesh['seq'=4,'table'=8] {'seq'}, dimensions={1}, use_global_device_ids=true | all-gather | bytes 655360 | tf_op jit(solution)/shard_map/all_gather | solution.py:83
  32.8 1.5 fusion.12
  35.0 0.0 copy-start.1
  35.0 5.2 %conditional.1 = (f32[128,512]{0,1:T(8,128)S(1)}, f32[128,512]{0,1:T(8,128)}, f32[512,512]{0,1:T(8,128)S(1)}) conditional(s32[]{:T(128)} %convert_element_type.42, f32[128,512]{0,1:T(8,128)S(1)} %broadcast_in_dim.54, (bf16[512,512]{0,1:T(8,128)(2,1)}, bf16[128,1536]{1,0:T(8,128)(2,1)S(1)}, bf16[512,512]{1,0:T(8,128)(2,1)S(1)}, f32[512,128]{1,0:T(8,128)}, ...), branch_computations={%region_5.6_spmd, %region_6.7_spmd} | conditional | flops 345243648 | bytes 21626960 | solution.py:116
  35.0 0.2 copy.29
  35.3 0.0 copy-start.6
  35.3 0.2 copy.30
  35.5 0.0 copy-start.7
  35.5 0.5 fusion.30
  36.0 0.2 copy-done.6
  36.3 0.3 copy-done.7
  36.5 1.2 multiply_convert_fusion.1
  37.7 0.3 fusion.32
  38.1 0.8 fusion
  38.9 0.8 bitcast_add_fusion
  39.7 0.5 fusion.31
  40.1 0.0 copy-start.4
  40.1 0.0 copy-start.2
  40.2 0.9 copy-done.4
  41.1 0.0 reduce-scatter.2.cloned.1.call-update
  41.1 0.7 fusion.23
  41.8 0.0 copy-done.1
  41.8 1.1 gather_fusion
  43.0 0.1 fusion.16
  43.1 0.2 reduce_window_sum.11
  43.2 1.1 gather_fusion.1
  44.4 0.2 select_reduce_fusion
  44.6 1.0 scatter_custom_fusion
  45.6 0.7 all_to_all.12
  46.2 4.9 %all-to-all-start = ((s32[8,1,32]{2,1,0:T(1,128)}), s32[8,1,32]{2,1,0:T(1,128)S(1)}, u32[]{:S(2)}, u32[]{:S(2)}) async-start(s32[8,1,32]{2,1,0:T(1,128)} %all_to_all.12), calls=%async_computation | async-start | bytes 8192 | tf_op jit(solution)/shard_map/all_to_all | solution.py:147
  51.1 1.0 convert.11
  52.1 17.2 %reduce-scatter.2.cloned.1.call-done = f32[128,512]{0,1:T(8,128)} async-done(((f32[512,512]{0,1:T(8,128)}), f32[128,512]{0,1:T(8,128)}) %reduce-scatter.2.cloned.1.call-update) | async-done | bytes 262160 | tf_op jit(solution)/shard_map/reduce_scatter | solution.py:121
  69.3 1.0 convert.9
  70.3 0.0 copy-start.9
  70.3 0.0 copy-start.5
  70.3 0.7 convolution_convert_fusion.2
  71.0 1.7 %scatter_custom_fusion.1 = bf16[256,512]{1,0:T(8,128)(2,1)} fusion(s32[128]{0:T(128)S(1)} %fusion.24, bf16[128,512]{1,0:T(8,128)(2,1)S(1)} %convolution_convert_fusion.2, bf16[]{:T(256)} %constant.58.clone.1), kind=kCustom, calls=%fused_computation.37 | custom fusion | bytes 262146 | tf_op jit(solution)/shard_map/scatter | solution.py:136
  72.7 0.0 all-to-all-done
  72.7 4.6 %all-to-all-start.1 = ((bf16[8,32,512]{2,1,0:T(8,128)(2,1)}), bf16[8,32,512]{2,1,0:T(8,128)(2,1)S(1)}, u32[]{:S(2)}, u32[]{:S(2)}) async-start(bf16[8,32,512]{2,1,0:T(8,128)(2,1)} %bitcast.16), calls=%async_computation.2 | async-start | bytes 524288 | tf_op jit(solution)/shard_map/all_to_all | solution.py:146
  77.3 0.0 all-reduce.2.cloned.1.call-start
  77.3 0.5 broadcast.247
  77.8 0.7 reduce.5
  78.5 0.1 eq.75
  78.6 8.4 %all-to-all-done.1 = bf16[8,32,512]{2,1,0:T(8,128)(2,1)S(1)} async-done(((bf16[8,32,512]{2,1,0:T(8,128)(2,1)}), bf16[8,32,512]{2,1,0:T(8,128)(2,1)S(1)}, u32[]{:S(2)}, u32[]{:S(2)}) %all-to-all-start.1) | async-done | bytes 262176 | tf_op jit(solution)/shard_map/all_to_all | solution.py:146
  87.0 1.1 convolution_convert_fusion.1
  88.1 0.0 all-reduce.2.cloned.1.call-update
  88.2 0.1 reshape.198
  88.3 43.3 %all-reduce.2.cloned.1.call-done = bf16[512,512]{1,0:T(8,128)(2,1)} async-done(((bf16[512,512]{1,0:T(8,128)(2,1)}), bf16[512,512]{1,0:T(8,128)(2,1)}) %all-reduce.2.cloned.1.call-update) | async-done | bytes 524304 | tf_op jit(solution)/shard_map/psum | solution.py:152
  131.6 1.2 fusion.4
  132.8 0.6 sqrt_add_fusion
  133.4 2.5 %subtract_convert_fusion = (bf16[512,512]{1,0:T(8,128)(2,1)S(1)}, f32[512,512]{1,0:T(8,128)}) fusion(bf16[512,512]{1,0:T(8,128)(2,1)} %param.19, f32[512]{0:T(512)S(1)} %get-tuple-element.118, bf16[512,512]{1,0:T(8,128)(2,1)} %all-reduce.2.cloned.1.call-done, f32[512,512]{1,0:T(8,128)S(1)} %copy-done.5), kind=kLoop, calls=%fused_computation.23 | loop fusion | flops 2359296 | bytes 3672064 | tf_op jit(solution)/shard_map/convert_element_type | solution.py:32
  135.9 1.2 gather_fusion.2
  137.1 0.8 broadcast_select_fusion
  137.9 4.6 %all-to-all-start.2 = ((bf16[8,32,512]{2,1,0:T(8,128)(2,1)}), bf16[8,32,512]{2,1,0:T(8,128)(2,1)S(1)}, u32[]{:S(2)}, u32[]{:S(2)}) async-start(bf16[8,32,512]{2,1,0:T(8,128)(2,1)} %broadcast_select_fusion), calls=%async_computation.3 | async-start | bytes 524288 | tf_op jit(solution)/shard_map/all_to_all | solution.py:158
  142.5 9.7 %all-to-all-done.2 = bf16[8,32,512]{2,1,0:T(8,128)(2,1)S(1)} async-done(((bf16[8,32,512]{2,1,0:T(8,128)(2,1)}), bf16[8,32,512]{2,1,0:T(8,128)(2,1)S(1)}, u32[]{:S(2)}, u32[]{:S(2)}) %all-to-all-start.2) | async-done | bytes 262176 | tf_op jit(solution)/shard_map/all_to_all | solution.py:158
  152.2 1.5 gather_fusion.3
  (21 shorter events, 0.2 us)
Async XLA Ops:
  7.2 1.4 copy-start
  7.2 14.2 %copy-start.8 = (bf16[1,128,512]{2,1,0:T(8,128)(2,1)S(1)}, bf16[1,128,512]{2,1,0:T(8,128)(2,1)}, u32[]{:S(2)}) copy-start(bf16[1,128,512]{2,1,0:T(8,128)(2,1)} %param.14) | copy-start | bytes 393220
  7.2 62.1 %reduce-scatter.2.cloned.1.call-start = ((), (), s32[]{:S(2)}) async-start(), calls=%async_computation.4 | async-start | bytes 1310720 | tf_op jit(solution)/shard_map/reduce_scatter | solution.py:121
  35.0 6.8 %copy-start.1 = (s32[4096]{0:T(1024)S(1)}, s32[4096]{0:T(1024)}, u32[]{:S(2)}) copy-start(s32[4096]{0:T(1024)} %param.17) | copy-start | bytes 49156
  35.3 1.0 copy-start.6
  35.5 1.1 copy-start.7
  40.1 1.0 copy-start.4
  40.1 3.1 %copy-start.2 = (s32[4096]{0:T(1024)S(1)}, s32[4096]{0:T(1024)}, u32[]{:S(2)}) copy-start(s32[4096]{0:T(1024)} %param.18) | copy-start | bytes 49156
  46.2 26.5 %all-to-all-start = ((s32[8,1,32]{2,1,0:T(1,128)}), s32[8,1,32]{2,1,0:T(1,128)S(1)}, u32[]{:S(2)}, u32[]{:S(2)}) async-start(s32[8,1,32]{2,1,0:T(1,128)} %all_to_all.12), calls=%async_computation | async-start | bytes 8192 | tf_op jit(solution)/shard_map/all_to_all | solution.py:147
  70.3 62.6 %copy-start.9 = (f32[512]{0:T(512)S(1)}, f32[512]{0:T(512)}, u32[]{:S(2)}) copy-start(f32[512]{0:T(512)} %param.21) | copy-start | bytes 6148
  70.3 63.1 %copy-start.5 = (f32[512,512]{1,0:T(8,128)S(1)}, f32[512,512]{1,0:T(8,128)}, u32[]{:S(2)}) copy-start(f32[512,512]{1,0:T(8,128)} %param.20) | copy-start | bytes 3145732
  72.7 14.3 %all-to-all-start.1 = ((bf16[8,32,512]{2,1,0:T(8,128)(2,1)}), bf16[8,32,512]{2,1,0:T(8,128)(2,1)S(1)}, u32[]{:S(2)}, u32[]{:S(2)}) async-start(bf16[8,32,512]{2,1,0:T(8,128)(2,1)} %bitcast.16), calls=%async_computation.2 | async-start | bytes 524288 | tf_op jit(solution)/shard_map/all_to_all | solution.py:146
  77.3 54.3 %all-reduce.2.cloned.1.call-start = ((), (), s32[]{:S(2)}) async-start(), calls=%async_computation.5 | async-start | bytes 1048576 | tf_op jit(solution)/shard_map/psum | solution.py:152
  135.9 17.8 %copy-start.3 = (bf16[512,512]{1,0:T(8,128)(2,1)}, bf16[512,512]{1,0:T(8,128)(2,1)S(1)}, u32[]{:S(2)}) copy-start(bf16[512,512]{1,0:T(8,128)(2,1)S(1)} %get-tuple-element.116) | copy-start | bytes 1572868
  137.9 14.3 %all-to-all-start.2 = ((bf16[8,32,512]{2,1,0:T(8,128)(2,1)}), bf16[8,32,512]{2,1,0:T(8,128)(2,1)S(1)}, u32[]{:S(2)}, u32[]{:S(2)}) async-start(bf16[8,32,512]{2,1,0:T(8,128)(2,1)} %broadcast_select_fusion), calls=%async_computation.3 | async-start | bytes 524288 | tf_op jit(solution)/shard_map/all_to_all | solution.py:158
Sparse Core Ops, SparseCore 0:
  41.3 27.9 reduce-scatter.1
  88.3 43.2 all-reduce.1
where the time goes:
time: 161 us
  waiting for transfers between devices  78.7 us (49%)
  blocking collectives  22.8 us (14%)
  between operations  14.9 us (9%)
  starting transfers between devices  14.2 us (9%)
  other arithmetic  12.2 us (8%)
  local copies, waits for them, and re-layouts  11.3 us (7%)
  matrix products  6.34 us (4%)
    psum x1, waiting for transfers between devices, body(): lax.psum(slab_grad.astype(jnp.bfloat16), 'seq').astype(jnp.float32)  43.3 us
    reduce_scatter x1, waiting for transfers between devices, body(): lax.psum_scatter(query_terms, 'seq', scatter_dimension=0, tiled=True)  17.2 us
    all_gather x1, blocking collectives, body(): query_piece = lax.all_gather(queries, 'seq', axis=0, tiled=True)  11.5 us
    all_gather x1, blocking collectives, body(): grad_piece = lax.all_gather(cotangent, 'seq', axis=0, tiled=True)  11.3 us
    all_to_all x1, waiting for transfers between devices, body(): lax.all_to_all(replies, 'table', split_axis=0, concat_axis=0, tiled=True)  9.73 us
    all_to_all x1, waiting for transfers between devices, body(): lax.all_to_all(send_rows, 'table', split_axis=0, concat_axis=0, tiled=True)  8.44 us
    all_to_all x1, starting transfers between devices, body(): lax.all_to_all(send_index, 'table', split_axis=0, concat_axis=0, tiled=True)  4.88 us
    all_to_all x1, starting transfers between devices, body(): lax.all_to_all(replies, 'table', split_axis=0, concat_axis=0, tiled=True)  4.61 us
  transfers between devices with their start and end apart: 5, of which 4 were waited for; matrix products, arithmetic and copies ran while one was open for 6% of the time, Pallas kernels for 0%

commit v1 on v0

v1 whole, which is shorter than its diff:
```python
import functools
import math

import jax
import jax.numpy as jnp
from jax import lax
from jax.experimental import pallas as pl
from jax.experimental.pallas import tpu as pltpu
from jax.sharding import PartitionSpec as P

HEADS = 8
LANES = 128

first_decay = 0.9
second_decay = 0.99
step_rate = 0.05
epsilon = 1e-08

F32 = jnp.float32
BF16 = jnp.bfloat16
MESH = pl.DeviceIdType.MESH


def iota(shape, axis):
    return lax.broadcasted_iota(jnp.int32, shape, axis)


def dot(a, b):
    return jnp.dot(a, b, preferred_element_type=F32)


def dot_nt(a, b):
    return lax.dot_general(a, b, (((1,), (1,)), ((), ())), preferred_element_type=F32)


def dot_tn(a, b):
    return lax.dot_general(a, b, (((0,), (0,)), ((), ())), preferred_element_type=F32)


def kernel(
    seq_count, owner_count, capacity,
    x_ref, proj_hbm, do_ref, mask_ref, ids_ref, owner_ref, local_ref, table_hbm, moment_hbm, second_ref,
    ntab_hbm, nmom_hbm, nsec_ref, event_ref,
    x_all, do_all, proj_ref, table_ref, moment_ref, ntab_ref, nmom_ref,
    own_ref, other_ref, dq_ref, dk_ref, dv_ref, sendsel_ref,
    idx_send, idx_got, idx_all, send_buf, got, grad_ref, reply_buf, returned,
    load_sem, store_sem, x_send, x_recv, do_send, do_recv, idx_ssem, idx_rsem, idxf_ssem, idxf_rsem,
    row_ssem, row_rsem, fwd_ssem, fwd_rsem, rep_ssem, rep_rsem,
):
    pos = lax.axis_index("seq")
    me = lax.axis_index("table")
    tokens, features = x_ref.shape
    head_size = features // HEADS
    slab_rows = table_ref.shape[0]
    width = owner_count * capacity
    history_scale = 1.0 / math.sqrt(tokens * seq_count)
    temper = 1.0 / math.sqrt(head_size)
    turn = 1 - 2 * (pos % 2)

    def seq_peer(r):
        return lax.rem(pos + turn * r + seq_count, seq_count)

    def table_peer(r):
        return lax.rem(me + r, owner_count)

    def rows_of(owner):
        return pl.ds(pl.multiple_of(owner * capacity, capacity), capacity)

    def to_seq(src, dst, ssem, rsem, peer):
        return pltpu.make_async_remote_copy(
            src_ref=src, dst_ref=dst, send_sem=ssem, recv_sem=rsem,
            device_id=(peer, me), device_id_type=MESH,
        )

    def to_table(src, dst, ssem, rsem, peer):
        return pltpu.make_async_remote_copy(
            src_ref=src, dst_ref=dst, send_sem=ssem, recv_sem=rsem,
            device_id=(pos, peer), device_id_type=MESH,
        )

    def each(first, last, step):
        lax.fori_loop(first, last, lambda r, c: (step(r), c)[1], 0)

    loads = [
        pltpu.make_async_copy(proj_hbm, proj_ref, load_sem.at[0]),
        pltpu.make_async_copy(table_hbm, table_ref, load_sem.at[1]),
        pltpu.make_async_copy(moment_hbm, moment_ref, load_sem.at[2]),
    ]
    for load in loads:
        load.start()

    barrier = pltpu.get_barrier_semaphore()

    def greet_seq(r):
        pl.semaphore_signal(barrier, inc=1, device_id=(seq_peer(r), me), device_id_type=MESH)

    def greet_table(r):
        pl.semaphore_signal(barrier, inc=1, device_id=(pos, table_peer(r)), device_id_type=MESH)

    each(1, seq_count, greet_seq)
    each(1, owner_count, greet_table)
    pl.semaphore_wait(barrier, seq_count + owner_count - 2)

    def x_copy(peer):
        return to_seq(x_ref, x_all.at[pos], x_send.at[peer], x_recv.at[pos], peer)

    def do_copy(peer):
        return to_seq(do_ref, do_all.at[pos], do_send.at[peer], do_recv.at[pos], peer)

    def send_block(r):
        peer = seq_peer(r)
        x_copy(peer).start()

        @pl.when(peer < pos)
        def _():
            do_copy(peer).start()

    each(1, seq_count, send_block)

    eye = iota((LANES, LANES), 0) == iota((LANES, LANES), 1)

    def to_col(row):
        return jnp.sum(jnp.where(eye, row, 0.0), axis=1, keepdims=True)

    def to_row(col):
        return jnp.sum(jnp.where(eye, col, 0.0), axis=0, keepdims=True)

    ids = ids_ref[...]
    high_col = to_col((ids // LANES).astype(F32))
    low_col = to_col((ids % LANES).astype(F32))
    id_rows = owner_ref.shape[0]
    local_ids = local_ref[...]
    parts = jnp.concatenate(
        [
            owner_ref[...].astype(F32).astype(BF16),
            (local_ids % 256).astype(F32).astype(BF16),
            (local_ids // 256).astype(F32).astype(BF16),
        ],
        axis=1,
    )
    pick = jnp.where(iota((tokens, id_rows), 1).astype(F32) == high_col, 1.0, 0.0).astype(BF16)
    found = dot(pick, parts)
    in_row = iota((tokens, LANES), 1).astype(F32) == low_col

    def column(part):
        piece = found[:, part * LANES : (part + 1) * LANES]
        return jnp.sum(jnp.where(in_row, piece, 0.0), axis=1, keepdims=True)

    owner_col = column(0)
    local_col = column(1) + 256.0 * column(2)
    owner_row = to_row(owner_col)
    before = (owner_col == owner_row) & (iota((tokens, tokens), 0) < iota((tokens, tokens), 1))
    slot_row = jnp.sum(jnp.where(before, 1.0, 0.0), axis=0, keepdims=True)
    slot_col = to_col(slot_row)
    target_row = owner_row * capacity + slot_row
    sendsel_ref[...] = jnp.where(
        iota((width, tokens), 0).astype(F32) == target_row, 1.0, 0.0
    ).astype(BF16)
    lane_col = slot_col + (me * capacity).astype(F32)
    marks = jnp.where(iota((tokens, width), 1).astype(F32) == lane_col, local_col + 1.0, 0.0)

    def make_index(owner):
        line = jnp.sum(
            jnp.where(owner_col == owner.astype(F32), marks, 0.0), axis=0, keepdims=True
        )
        idx_send[owner] = jnp.broadcast_to(line, (8, width))

    each(0, owner_count, make_index)

    def idx_copy(peer):
        return to_table(
            idx_send.at[peer], idx_got.at[me], idx_ssem.at[peer], idx_rsem.at[me], peer
        )

    each(1, owner_count, lambda r: idx_copy(table_peer(r)).start())
    idx_got[me] = idx_send[me]

    x_all[pos] = x_ref[...]
    do_all[pos] = do_ref[...]
    loads[0].wait()
    own_ref[...] = dot(x_ref[...], proj_ref[...]).astype(BF16)
    dq_ref[...] = jnp.zeros_like(dq_ref)
    dk_ref[...] = jnp.zeros_like(dk_ref)
    dv_ref[...] = jnp.zeros_like(dv_ref)

    lane = iota((1, LANES), 1)
    group = LANES // head_size
    span = group * tokens
    head_masks = [
        jnp.where(lane // head_size == g, 1.0, 0.0).astype(BF16) for g in range(group)
    ]

    def spread(block):
        return jnp.concatenate([block * m for m in head_masks], axis=0)

    def terms(scores_dot, grad_dot, allowed):
        scores = scores_dot * temper
        gates = 0.5 * jnp.tanh(0.5 * scores) + 0.5
        scaled = gates * allowed
        weights = (scores * scaled).astype(BF16)
        slopes = scaled * (1.0 + scores * (1.0 - gates))
        score_grad = (grad_dot * slopes * temper).astype(BF16)
        return weights, score_grad

    row_ids = iota((tokens, span), 0)
    lane_ids = iota((tokens, span), 1) % tokens

    def visible(query_block, key_block):
        seen = mask_ref[query_block, key_block] == 1
        return jnp.where(seen | (query_block == key_block), history_scale, 0.0)

    def block_step(r):
        block = seq_peer(r)

        @pl.when(r > 0)
        def _():
            to_seq(
                x_all.at[block], x_all.at[block], x_send.at[block], x_recv.at[block], block
            ).wait_recv()

        @pl.when(block <= pos)
        def _():
            @pl.when(block < pos)
            def _():
                other_ref[...] = dot(x_all[block], proj_ref[:, features:]).astype(BF16)

            @pl.when(block == pos)
            def _():
                other_ref[...] = own_ref[:, features:]

            allowed = jnp.where(
                lane_ids <= row_ids + (pos - block) * tokens, visible(pos, block), 0.0
            )
            for c in range(features // LANES):
                cols = slice(c * LANES, (c + 1) * LANES)
                keys = spread(other_ref[:, cols])
                values = spread(other_ref[:, features + c * LANES : features + (c + 1) * LANES])
                _, score_grad = terms(
                    dot_nt(own_ref[:, cols], keys), dot_nt(do_ref[:, cols], values), allowed
                )
                dq_ref[:, cols] += dot(score_grad, keys)

        @pl.when(block >= pos)
        def _():
            @pl.when(block > pos)
            def _():
                to_seq(
                    do_all.at[block], do_all.at[block], do_send.at[block], do_recv.at[block], block
                ).wait_recv()
                other_ref[:, :features] = dot(x_all[block], proj_ref[:, :features]).astype(BF16)

            @pl.when(block == pos)
            def _():
                other_ref[:, :features] = own_ref[:, :features]

            allowed = jnp.where(
                row_ids <= lane_ids + (block - pos) * tokens, visible(block, pos), 0.0
            )
            for c in range(features // LANES):
                cols = slice(c * LANES, (c + 1) * LANES)
                queries = spread(other_ref[:, cols])
                grads = spread(do_all[block, :, cols])
                weights, score_grad = terms(
                    dot_nt(own_ref[:, features + c * LANES : features + (c + 1) * LANES], queries),
                    dot_nt(
                        own_ref[:, 2 * features + c * LANES : 2 * features + (c + 1) * LANES], grads
                    ),
                    allowed,
                )
                dk_ref[:, cols] += dot(score_grad, queries)
                dv_ref[:, cols] += dot(weights, grads)

    each(0, seq_count, block_step)

    def take_index(r):
        peer = table_peer(r)
        to_table(
            idx_got.at[peer], idx_got.at[peer], idx_ssem.at[peer], idx_rsem.at[peer], peer
        ).wait_recv()

    each(1, owner_count, take_index)
    idx_all[pos] = jnp.sum(idx_got[...], axis=0)

    def idxf_copy(peer):
        return to_seq(idx_all.at[pos], idx_all.at[pos], idxf_ssem.at[peer], idxf_rsem.at[pos], peer)

    each(1, seq_count, lambda r: idxf_copy(seq_peer(r)).start())

    stacked = jnp.concatenate(
        [dq_ref[...].astype(BF16), dk_ref[...].astype(BF16), dv_ref[...].astype(BF16)], axis=1
    )
    input_grad = dot_nt(stacked, proj_ref[...]).astype(BF16)
    send_buf[...] = dot(sendsel_ref[...], input_grad).astype(BF16)

    def row_copy(peer):
        return to_table(
            send_buf.at[rows_of(peer)], got.at[pos, rows_of(me)],
            row_ssem.at[peer], row_rsem.at[me], peer,
        )

    each(1, owner_count, lambda r: row_copy(table_peer(r)).start())
    got[pos, rows_of(me)] = send_buf[rows_of(me)]

    def forward(source):
        def one(r):
            peer = seq_peer(r)
            to_seq(
                got.at[pos, rows_of(source)], got.at[pos, rows_of(source)],
                fwd_ssem.at[peer], fwd_rsem.at[pos], peer,
            ).start()

        each(1, seq_count, one)

    forward(me)

    def relay(r):
        source = lax.rem(me - r + owner_count, owner_count)
        part = got.at[pos, rows_of(source)]
        to_table(part, part, row_ssem.at[source], row_rsem.at[source], source).wait_recv()
        forward(source)

    each(1, owner_count, relay)

    slab_ids = iota((slab_rows, width), 0).astype(F32) + 1.0

    def select(block):
        return jnp.where(slab_ids == idx_all[block][0:1, :], 1.0, 0.0).astype(BF16)

    grad_ref[...] = dot(select(pos), got[pos])

    def add_block(r):
        block = seq_peer(r)
        to_seq(
            idx_all.at[block], idx_all.at[block], idxf_ssem.at[block], idxf_rsem.at[block], block
        ).wait_recv()
        to_seq(
            got.at[block], got.at[block], fwd_ssem.at[block], fwd_rsem.at[block], block
        ).wait_recv()
        grad_ref[...] += dot(select(block), got[block])

    each(1, seq_count, add_block)

    loads[1].wait()
    loads[2].wait()
    for c in range(slab_rows // LANES):
        rows = slice(c * LANES, (c + 1) * LANES)
        grad = grad_ref[rows, :]
        new_moment = first_decay * moment_ref[rows, :] + (1.0 - first_decay) * grad
        mean_square = jnp.sum(grad * grad, axis=1, keepdims=True) * (1.0 / features)
        new_second = second_decay * to_col(second_ref[c : c + 1, :]) + (
            1.0 - second_decay
        ) * mean_square
        nsec_ref[c : c + 1, :] = to_row(new_second)
        nmom_ref[rows, :] = new_moment
        factor = step_rate / (jnp.sqrt(new_second) + epsilon)
        ntab_ref[rows, :] = (table_ref[rows, :].astype(F32) - new_moment * factor).astype(BF16)

    reply_buf[...] = dot_tn(select(pos), ntab_ref[...]).astype(BF16)

    def reply_copy(peer):
        return to_table(
            reply_buf.at[rows_of(peer)], returned.at[rows_of(me)],
            rep_ssem.at[peer], rep_rsem.at[me], peer,
        )

    each(1, owner_count, lambda r: reply_copy(table_peer(r)).start())
    stores = [
        pltpu.make_async_copy(nmom_ref, nmom_hbm, store_sem.at[0]),
        pltpu.make_async_copy(ntab_ref, ntab_hbm, store_sem.at[1]),
    ]
    for store in stores:
        store.start()
    returned[rows_of(me)] = reply_buf[rows_of(me)]

    def end_seq(r):
        peer = seq_peer(r)
        x_copy(peer).wait_send()

        @pl.when(peer < pos)
        def _():
            do_copy(peer).wait_send()

        idxf_copy(peer).wait_send()
        to_seq(got.at[pos], got.at[pos], fwd_ssem.at[peer], fwd_rsem.at[pos], peer).wait_send()

    each(1, seq_count, end_seq)

    def end_table(r):
        peer = table_peer(r)
        idx_copy(peer).wait_send()
        row_copy(peer).wait_send()
        part = returned.at[rows_of(peer)]
        to_table(part, part, rep_ssem.at[peer], rep_rsem.at[peer], peer).wait_recv()

    each(1, owner_count, end_table)
    event_ref[...] = dot_tn(sendsel_ref[...], returned[...]).astype(BF16)
    each(1, owner_count, lambda r: reply_copy(table_peer(r)).wait_send())
    for store in stores:
        store.wait()


def body(events_x, proj, out_grad, block_mask, item_ids, owner_of, local_of, table, moment, second):
    tokens, features = events_x.shape[1:]
    seq_count = lax.axis_size("seq")
    owner_count = lax.axis_size("table")
    slab_rows = table.shape[0]
    capacity = max(2 * tokens // owner_count, 16)
    width = owner_count * capacity
    vmem = pl.BlockSpec(memory_space=pltpu.VMEM)
    smem = pl.BlockSpec(memory_space=pltpu.SMEM)
    hbm = pl.BlockSpec(memory_space=pl.ANY)
    dma = pltpu.SemaphoreType.DMA
    new_table, new_moment, new_second, event_rows = pl.pallas_call(
        functools.partial(kernel, seq_count, owner_count, capacity),
        out_shape=(
            jax.ShapeDtypeStruct((slab_rows, features), BF16),
            jax.ShapeDtypeStruct((slab_rows, features), F32),
            jax.ShapeDtypeStruct((slab_rows // LANES, LANES), F32),
            jax.ShapeDtypeStruct((tokens, features), BF16),
        ),
        in_specs=[vmem, hbm, vmem, smem, vmem, vmem, vmem, hbm, hbm, vmem],
        out_specs=(hbm, hbm, vmem, vmem),
        scratch_shapes=[
            pltpu.VMEM((seq_count, tokens, features), BF16),
            pltpu.VMEM((seq_count, tokens, features), BF16),
            pltpu.VMEM(proj.shape, BF16),
            pltpu.VMEM((slab_rows, features), BF16),
            pltpu.VMEM((slab_rows, features), F32),
            pltpu.VMEM((slab_rows, features), BF16),
            pltpu.VMEM((slab_rows, features), F32),
            pltpu.VMEM((tokens, 3 * features), BF16),
            pltpu.VMEM((tokens, 2 * features), BF16),
            pltpu.VMEM((tokens, features), F32),
            pltpu.VMEM((tokens, features), F32),
            pltpu.VMEM((tokens, features), F32),
            pltpu.VMEM((width, tokens), BF16),
            pltpu.VMEM((owner_count, 8, width), F32),
            pltpu.VMEM((owner_count, 8, width), F32),
            pltpu.VMEM((seq_count, 8, width), F32),
            pltpu.VMEM((width, features), BF16),
            pltpu.VMEM((seq_count, width, features), BF16),
            pltpu.VMEM((slab_rows, features), F32),
            pltpu.VMEM((width, features), BF16),
            pltpu.VMEM((width, features), BF16),
            dma((3,)),
            dma((2,)),
            dma((seq_count,)),
            dma((seq_count,)),
            dma((seq_count,)),
            dma((seq_count,)),
            dma((owner_count,)),
            dma((owner_count,)),
            dma((seq_count,)),
            dma((seq_count,)),
            dma((owner_count,)),
            dma((owner_count,)),
            dma((seq_count,)),
            dma((seq_count,)),
            dma((owner_count,)),
            dma((owner_count,)),
        ],
        compiler_params=pltpu.CompilerParams(
            collective_id=0, has_side_effects=True, vmem_limit_bytes=48 * 1024 * 1024
        ),
    )(
        events_x[0],
        proj,
        out_grad[0],
        block_mask,
        item_ids,
        owner_of.reshape(-1, LANES),
        local_of.reshape(-1, LANES),
        table,
        moment,
        second.reshape(-1, LANES),
    )
    return (new_table, new_moment, new_second.reshape(-1), event_rows[None])


def solution(mesh):
    return jax.shard_map(
        body,
        mesh=mesh,
        in_specs=(
            P("table", "seq", None),
            P(),
            P("table", "seq", None),
            P(),
            P("table", "seq"),
            P(),
            P(),
            P("table", None),
            P("table", None),
            P("table"),
        ),
        out_specs=(P("table", None), P("table", None), P("table"), P("table", "seq", None)),
        check_vma=False,
    )
```

time: 161 us -> 58.5 us (0.36)
  waiting for transfers between devices: 78.7 us -> 0 us
  Pallas kernels: 0 us -> 45.5 us
  blocking collectives: 22.8 us -> 0 us
  between operations: 14.9 us -> 0.66 us
  starting transfers between devices: 14.2 us -> 0 us
  other arithmetic: 12.2 us -> 0 us
  matrix products: 6.34 us -> 0 us
    pallas_call x0 -> x1, Pallas kernels: none -> 45.5 us  [body(): pl.pallas_call(functools.partial(kernel, seq_count, owner_count, capacity...]
    psum x1 -> x0, waiting for transfers between devices: 43.3 us -> none  [body(): lax.psum(slab_grad.astype(jnp.bfloat16), 'seq').astype(jnp.float32)]
    all_gather x2 -> x0, blocking collectives: 22.8 us -> none  [the longest x1 11.5 us: body(): query_piece = lax.all_gather(queries, 'seq', axis=0, tiled=True)]
    all_to_all x3 -> x0, waiting for transfers between devices: 18.2 us -> none  [the longest x1 9.73 us: body(): lax.all_to_all(replies, 'table', split_axis=0, concat_axis=0, tiled=True)]
    reduce_scatter x1 -> x0, waiting for transfers between devices: 17.2 us -> none  [body(): lax.psum_scatter(query_terms, 'seq', scatter_dimension=0, tiled=True)]
    all_to_all x3 -> x0, starting transfers between devices: 14.1 us -> none  [the longest x1 4.88 us: body(): lax.all_to_all(send_index, 'table', split_axis=0, concat_axis=0, tiled=True)]
    unnamed x17 -> x24, local copies, waits for them, and re-layouts: 1.36 us -> 11.9 us
    dot_general x8 -> x0, matrix products: 6.34 us -> none  [the longest x1 1.27 us: body(): jnp.dot(inputs, proj, preferred_element_type=jnp.float32)]
  transfers between devices with their start and end apart: 5 -> 0, of which waited for: 4 -> 0; matrix products, arithmetic and copies ran while one was open for 6% -> 0% of each run, Pallas kernels for 0% -> 0%
where the time goes in v1:
time: 58.5 us; the launch traced here: 58.1 us
  Pallas kernels  45.5 us (78%)
  local copies, waits for them, and re-layouts  11.9 us (20%)
  between operations  0.66 us (1%)
    pallas_call x1, Pallas kernels, body(): pl.pallas_call(functools.partial(kernel, seq_count, owner_count, capacity...  45.5 us
    unnamed x24, local copies, waits for them, and re-layouts  11.9 us

profile of v1, /device:TPU:0, one launch (start us, length us, event | category | flops | bytes accessed | tf_op | source)
XLA Modules:
  0.0 58.1 jit_solution(5382902508831575549)
XLA Ops:
  0.6 0.0 copy-start
  0.6 1.4 %copy-done = bf16[512,1536]{1,0:T(8,128)(2,1)S(1)} copy-done((bf16[512,1536]{1,0:T(8,128)(2,1)S(1)}, bf16[512,1536]{1,0:T(8,128)(2,1)}, u32[]{:S(2)}) %copy-start) | copy-done | bytes 1572888
  2.0 0.0 copy-start.1
  2.0 1.2 %copy-done.1 = f32[512,512]{1,0:T(8,128)S(1)} copy-done((f32[512,512]{1,0:T(8,128)S(1)}, f32[512,512]{1,0:T(8,128)}, u32[]{:S(2)}) %copy-start.1) | copy-done | bytes 1048600
  3.3 0.0 copy-start.2
  3.3 1.0 %copy-done.2 = bf16[512,512]{1,0:T(8,128)(2,1)S(1)} copy-done((bf16[512,512]{1,0:T(8,128)(2,1)S(1)}, bf16[512,512]{1,0:T(8,128)(2,1)}, u32[]{:S(2)}) %copy-start.2) | copy-done | bytes 524312
  4.3 0.0 copy-start.3
  4.3 0.9 %copy-done.3 = bf16[1,128,512]{2,1,0:T(8,128)(2,1)S(1)} copy-done((bf16[1,128,512]{2,1,0:T(8,128)(2,1)S(1)}, bf16[1,128,512]{2,1,0:T(8,128)(2,1)}, u32[]{:S(2)}) %copy-start.3) | copy-done | bytes 131096
  5.2 0.0 copy-start.4
  5.2 0.9 %copy-done.4 = bf16[1,128,512]{2,1,0:T(8,128)(2,1)S(1)} copy-done((bf16[1,128,512]{2,1,0:T(8,128)(2,1)S(1)}, bf16[1,128,512]{2,1,0:T(8,128)(2,1)}, u32[]{:S(2)}) %copy-start.4) | copy-done | bytes 131096
  6.1 0.0 copy-start.5
  6.1 0.7 %copy-done.5 = s32[4096]{0:T(1024)S(1)} copy-done((s32[4096]{0:T(1024)S(1)}, s32[4096]{0:T(1024)}, u32[]{:S(2)}) %copy-start.5) | copy-done | bytes 16408
  6.8 0.0 copy-start.6
  6.8 0.7 %copy-done.6 = s32[4096]{0:T(1024)S(1)} copy-done((s32[4096]{0:T(1024)S(1)}, s32[4096]{0:T(1024)}, u32[]{:S(2)}) %copy-start.6) | copy-done | bytes 16408
  7.6 0.0 copy-start.7
  7.6 0.7 %copy-done.7 = s32[4,4]{1,0:T(4,128)S(1)} copy-done((s32[4,4]{1,0:T(4,128)S(1)}, s32[4,4]{1,0:T(4,128)}, u32[]{:S(2)}) %copy-start.7) | copy-done | bytes 88
  8.2 0.0 copy-start.8
  8.2 0.7 %copy-done.8 = f32[512]{0:T(512)S(1)} copy-done((f32[512]{0:T(512)S(1)}, f32[512]{0:T(512)}, u32[]{:S(2)}) %copy-start.8) | copy-done | bytes 2072
  8.9 0.0 copy-start.9
  8.9 0.7 %copy-done.9 = s32[1,128]{1,0:T(1,128)S(1)} copy-done((s32[1,128]{1,0:T(1,128)S(1)}, s32[1,128]{1,0:T(1,128)}, u32[]{:S(2)}) %copy-start.9) | copy-done | bytes 536
  9.6 45.5 %shard_map.129 = (bf16[512,512]{1,0:T(8,128)(2,1)S(1)}, f32[512,512]{1,0:T(8,128)S(1)}, f32[4,128]{1,0:T(4,128)S(1)}, bf16[128,512]{1,0:T(8,128)(2,1)S(1)}) custom-call(bf16[128,512]{1,0:T(8,128)(2,1)S(1)} %bitcast.7, bf16[512,1536]{1,0:T(8,128)(2,1)S(1)} %copy-done, bf16[128,512]{1,0:T(8,128)(2,1)S(1)} %bitcast.8, s32[4,4]{1,0:T(4,128)S(1)} %copy-done.7, ...), custom_call_target="tpu_custom_call" | custom-call | tf_op jit(solution)/shard_map/pallas_call | solution.py:413
  55.1 0.8 %copy.18 = bf16[512,512]{1,0:T(8,128)(2,1)} copy(bf16[512,512]{1,0:T(8,128)(2,1)S(1)} %get-tuple-element.16) | data formatting | bytes 1048576
  55.9 1.0 %copy.19 = f32[512,512]{1,0:T(8,128)} copy(f32[512,512]{1,0:T(8,128)S(1)} %get-tuple-element.17) | data formatting | bytes 2097152
  56.9 0.6 copy.20
  57.4 0.7 %copy.21 = bf16[1,128,512]{2,1,0:T(8,128)(2,1)} copy(bf16[1,128,512]{2,1,0:T(8,128)(2,1)S(1)} %bitcast.9) | data formatting | bytes 262144
Async XLA Ops:
  0.6 1.4 %copy-start = (bf16[512,1536]{1,0:T(8,128)(2,1)S(1)}, bf16[512,1536]{1,0:T(8,128)(2,1)}, u32[]{:S(2)}) copy-start(bf16[512,1536]{1,0:T(8,128)(2,1)} %proj_hbm.1) | copy-start | bytes 4718596
  2.0 1.2 %copy-start.1 = (f32[512,512]{1,0:T(8,128)S(1)}, f32[512,512]{1,0:T(8,128)}, u32[]{:S(2)}) copy-start(f32[512,512]{1,0:T(8,128)} %moment_hbm.1) | copy-start | bytes 3145732
  3.3 1.0 %copy-start.2 = (bf16[512,512]{1,0:T(8,128)(2,1)S(1)}, bf16[512,512]{1,0:T(8,128)(2,1)}, u32[]{:S(2)}) copy-start(bf16[512,512]{1,0:T(8,128)(2,1)} %table_hbm.1) | copy-start | bytes 1572868
  4.3 0.9 %copy-start.3 = (bf16[1,128,512]{2,1,0:T(8,128)(2,1)S(1)}, bf16[1,128,512]{2,1,0:T(8,128)(2,1)}, u32[]{:S(2)}) copy-start(bf16[1,128,512]{2,1,0:T(8,128)(2,1)} %param.10) | copy-start | bytes 393220
  5.2 0.9 %copy-start.4 = (bf16[1,128,512]{2,1,0:T(8,128)(2,1)S(1)}, bf16[1,128,512]{2,1,0:T(8,128)(2,1)}, u32[]{:S(2)}) copy-start(bf16[1,128,512]{2,1,0:T(8,128)(2,1)} %param.12) | copy-start | bytes 393220
  6.1 0.7 %copy-start.5 = (s32[4096]{0:T(1024)S(1)}, s32[4096]{0:T(1024)}, u32[]{:S(2)}) copy-start(s32[4096]{0:T(1024)} %param.15) | copy-start | bytes 49156
  6.8 0.7 %copy-start.6 = (s32[4096]{0:T(1024)S(1)}, s32[4096]{0:T(1024)}, u32[]{:S(2)}) copy-start(s32[4096]{0:T(1024)} %param.16) | copy-start | bytes 49156
  7.6 0.7 %copy-start.7 = (s32[4,4]{1,0:T(4,128)S(1)}, s32[4,4]{1,0:T(4,128)}, u32[]{:S(2)}) copy-start(s32[4,4]{1,0:T(4,128)} %mask_ref.1) | copy-start | bytes 196
  8.2 0.7 %copy-start.8 = (f32[512]{0:T(512)S(1)}, f32[512]{0:T(512)}, u32[]{:S(2)}) copy-start(f32[512]{0:T(512)} %param.19) | copy-start | bytes 6148
  8.9 0.7 %copy-start.9 = (s32[1,128]{1,0:T(1,128)S(1)}, s32[1,128]{1,0:T(1,128)}, u32[]{:S(2)}) copy-start(s32[1,128]{1,0:T(1,128)} %ids_ref.1) | copy-start | bytes 1540

commit v2 on v1

--- a/solution.py
+++ b/solution.py
@@ -10,6 +10,7 @@
 
 HEADS = 8
 LANES = 128
+VMEM_BYTES = 63 * 1024 * 1024
 
 first_decay = 0.9
 second_decay = 0.99
@@ -39,8 +40,9 @@
 
 def kernel(
     seq_count, owner_count, capacity,
-    x_ref, proj_hbm, do_ref, mask_ref, ids_ref, owner_ref, local_ref, table_hbm, moment_hbm, second_ref,
-    ntab_hbm, nmom_hbm, nsec_ref, event_ref,
+    x_hbm, proj_hbm, do_hbm, mask_ref, ids_hbm, owner_hbm, local_hbm, table_hbm, moment_hbm, second_hbm,
+    ntab_hbm, nmom_hbm, nsec_hbm, event_hbm,
+    x_ref, do_ref, ids_ref, owner_ref, local_ref, second_ref, nsec_ref, event_ref,
     x_all, do_all, proj_ref, table_ref, moment_ref, ntab_ref, nmom_ref,
     own_ref, other_ref, dq_ref, dk_ref, dv_ref, sendsel_ref,
     idx_send, idx_got, idx_all, send_buf, got, grad_ref, reply_buf, returned,
@@ -82,9 +84,20 @@
         lax.fori_loop(first, last, lambda r, c: (step(r), c)[1], 0)
 
     loads = [
-        pltpu.make_async_copy(proj_hbm, proj_ref, load_sem.at[0]),
-        pltpu.make_async_copy(table_hbm, table_ref, load_sem.at[1]),
-        pltpu.make_async_copy(moment_hbm, moment_ref, load_sem.at[2]),
+        pltpu.make_async_copy(source, target, load_sem.at[number])
+        for number, (source, target) in enumerate(
+            [
+                (ids_hbm, ids_ref),
+                (owner_hbm, owner_ref),
+                (local_hbm, local_ref),
+                (x_hbm, x_ref),
+                (do_hbm, do_ref),
+                (proj_hbm, proj_ref),
+                (table_hbm, table_ref),
+                (moment_hbm, moment_ref),
+                (second_hbm, second_ref),
+            ]
+        )
     ]
     for load in loads:
         load.start()
@@ -102,10 +115,10 @@
     pl.semaphore_wait(barrier, seq_count + owner_count - 2)
 
     def x_copy(peer):
-        return to_seq(x_ref, x_all.at[pos], x_send.at[peer], x_recv.at[pos], peer)
+        return to_seq(x_hbm, x_all.at[pos], x_send.at[peer], x_recv.at[pos], peer)
 
     def do_copy(peer):
-        return to_seq(do_ref, do_all.at[pos], do_send.at[peer], do_recv.at[pos], peer)
+        return to_seq(do_hbm, do_all.at[pos], do_send.at[peer], do_recv.at[pos], peer)
 
     def send_block(r):
         peer = seq_peer(r)
@@ -125,6 +138,8 @@
     def to_row(col):
         return jnp.sum(jnp.where(eye, col, 0.0), axis=0, keepdims=True)
 
+    for load in loads[:3]:
+        load.wait()
     ids = ids_ref[...]
     high_col = to_col((ids // LANES).astype(F32))
     low_col = to_col((ids % LANES).astype(F32))
@@ -175,9 +190,10 @@
     each(1, owner_count, lambda r: idx_copy(table_peer(r)).start())
     idx_got[me] = idx_send[me]
 
+    for load in loads[3:6]:
+        load.wait()
     x_all[pos] = x_ref[...]
     do_all[pos] = do_ref[...]
-    loads[0].wait()
     own_ref[...] = dot(x_ref[...], proj_ref[...]).astype(BF16)
     dq_ref[...] = jnp.zeros_like(dq_ref)
     dk_ref[...] = jnp.zeros_like(dk_ref)
@@ -340,8 +356,8 @@
 
     each(1, seq_count, add_block)
 
-    loads[1].wait()
-    loads[2].wait()
+    for load in loads[6:]:
+        load.wait()
     for c in range(slab_rows // LANES):
         rows = slice(c * LANES, (c + 1) * LANES)
         grad = grad_ref[rows, :]
@@ -367,6 +383,7 @@
     stores = [
         pltpu.make_async_copy(nmom_ref, nmom_hbm, store_sem.at[0]),
         pltpu.make_async_copy(ntab_ref, ntab_hbm, store_sem.at[1]),
+        pltpu.make_async_copy(nsec_ref, nsec_hbm, store_sem.at[2]),
     ]
     for store in stores:
         store.start()
@@ -394,9 +411,31 @@
 
     each(1, owner_count, end_table)
     event_ref[...] = dot_tn(sendsel_ref[...], returned[...]).astype(BF16)
+    last = pltpu.make_async_copy(event_ref, event_hbm, store_sem.at[3])
+    last.start()
     each(1, owner_count, lambda r: reply_copy(table_peer(r)).wait_send())
     for store in stores:
         store.wait()
+    last.wait()
+
+
+def pass_on(*refs):
+    sems = refs[-1]
+    half = len(refs) // 2
+    copies = []
+    for source, target in zip(refs[:half], refs[half:-1]):
+        rows = source.shape[0]
+        pieces = rows // LANES if rows > LANES else 1
+        size = rows // pieces
+        for piece in range(pieces):
+            part = pl.ds(piece * size, size)
+            copies.append(
+                pltpu.make_async_copy(source.at[part], target.at[part], sems.at[len(copies)])
+            )
+    for copy in copies:
+        copy.start()
+    for copy in copies:
+        copy.wait()
 
 
 def body(events_x, proj, out_grad, block_mask, item_ids, owner_of, local_of, table, moment, second):
@@ -406,11 +445,10 @@
     slab_rows = table.shape[0]
     capacity = max(2 * tokens // owner_count, 16)
     width = owner_count * capacity
-    vmem = pl.BlockSpec(memory_space=pltpu.VMEM)
     smem = pl.BlockSpec(memory_space=pltpu.SMEM)
     hbm = pl.BlockSpec(memory_space=pl.ANY)
     dma = pltpu.SemaphoreType.DMA
-    new_table, new_moment, new_second, event_rows = pl.pallas_call(
+    results = pl.pallas_call(
         functools.partial(kernel, seq_count, owner_count, capacity),
         out_shape=(
             jax.ShapeDtypeStruct((slab_rows, features), BF16),
@@ -418,9 +456,17 @@
             jax.ShapeDtypeStruct((slab_rows // LANES, LANES), F32),
             jax.ShapeDtypeStruct((tokens, features), BF16),
         ),
-        in_specs=[vmem, hbm, vmem, smem, vmem, vmem, vmem, hbm, hbm, vmem],
-        out_specs=(hbm, hbm, vmem, vmem),
+        in_specs=[hbm, hbm, hbm, smem] + [hbm] * 6,
+        out_specs=(hbm,) * 4,
         scratch_shapes=[
+            pltpu.VMEM((tokens, features), BF16),
+            pltpu.VMEM((tokens, features), BF16),
+            pltpu.VMEM((1, tokens), jnp.int32),
+            pltpu.VMEM((owner_of.shape[0] // LANES, LANES), jnp.int32),
+            pltpu.VMEM((owner_of.shape[0] // LANES, LANES), jnp.int32),
+            pltpu.VMEM((slab_rows // LANES, LANES), F32),
+            pltpu.VMEM((slab_rows // LANES, LANES), F32),
+            pltpu.VMEM((tokens, features), BF16),
             pltpu.VMEM((seq_count, tokens, features), BF16),
             pltpu.VMEM((seq_count, tokens, features), BF16),
             pltpu.VMEM(proj.shape, BF16),
@@ -442,8 +488,8 @@
             pltpu.VMEM((slab_rows, features), F32),
             pltpu.VMEM((width, features), BF16),
             pltpu.VMEM((width, features), BF16),
-            dma((3,)),
-            dma((2,)),
+            dma((9,)),
+            dma((4,)),
             dma((seq_count,)),
             dma((seq_count,)),
             dma((seq_count,)),
@@ -460,7 +506,7 @@
             dma((owner_count,)),
         ],
         compiler_params=pltpu.CompilerParams(
-            collective_id=0, has_side_effects=True, vmem_limit_bytes=48 * 1024 * 1024
+            collective_id=0, has_side_effects=True, vmem_limit_bytes=VMEM_BYTES
         ),
     )(
         events_x[0],
@@ -474,6 +520,14 @@
         moment,
         second.reshape(-1, LANES),
     )
+    new_table, new_moment, new_second, event_rows = pl.pallas_call(
+        pass_on,
+        out_shape=tuple(jax.ShapeDtypeStruct(r.shape, r.dtype) for r in results),
+        in_specs=[hbm] * 4,
+        out_specs=(hbm,) * 4,
+        scratch_shapes=[dma((2 * (slab_rows // LANES) + 2,))],
+        compiler_params=pltpu.CompilerParams(vmem_limit_bytes=VMEM_BYTES),
+    )(*results)
     return (new_table, new_moment, new_second.reshape(-1), event_rows[None])
 
 

time: 58.5 us -> 100 us (1.71)
  Pallas kernels: 45.5 us -> 99.2 us
  local copies, waits for them, and re-layouts: 11.9 us -> 0 us
    pallas_call x0 -> x1, Pallas kernels: none -> 52.9 us  [body(): pl.pallas_call(pass_on, out_shape=tuple((jax.ShapeDtypeStruct(r.shape, r....]
    unnamed x24 -> x0, local copies, waits for them, and re-layouts: 11.9 us -> none
where the time goes in v2:
time: 100 us; the launch traced here: 99.8 us
  Pallas kernels  99.2 us (99%)
    pallas_call x1, Pallas kernels, body(): pl.pallas_call(pass_on, out_shape=tuple((jax.ShapeDtypeStruct(r.shape, r....  52.9 us
    pallas_call x1, Pallas kernels, body(): pl.pallas_call(functools.partial(kernel, seq_count, owner_count, capacity...  46.3 us

profile of v2, /device:TPU:0, one launch (start us, length us, event | category | flops | bytes accessed | tf_op | source)
XLA Modules:
  0.0 99.8 jit_solution(9680391417982691845)
XLA Ops:
  0.6 46.3 %shard_map.129 = (bf16[512,512]{1,0:T(8,128)(2,1)}, f32[512,512]{1,0:T(8,128)}, f32[4,128]{1,0:T(4,128)}, bf16[128,512]{1,0:T(8,128)(2,1)}) custom-call(bf16[128,512]{1,0:T(8,128)(2,1)} %bitcast.7, bf16[512,1536]{1,0:T(8,128)(2,1)} %proj_hbm.1, bf16[128,512]{1,0:T(8,128)(2,1)} %bitcast.8, s32[4,4]{1,0:T(4,128)} %mask_ref.1, s32[1,128]{1,0:T(1,128)} %ids_hbm.1, ...), custom_call_target="tpu_custom_call" | custom-call | tf_op jit(solution)/shard_map/pallas_call | solution.py:451
  46.9 52.9 %shard_map.130 = (bf16[512,512]{1,0:T(8,128)(2,1)}, f32[512,512]{1,0:T(8,128)}, f32[4,128]{1,0:T(4,128)}, bf16[128,512]{1,0:T(8,128)(2,1)}) custom-call(bf16[512,512]{1,0:T(8,128)(2,1)} %get-tuple-element.12.refs_0_, f32[512,512]{1,0:T(8,128)} %get-tuple-element.13.refs_1_, f32[4,128]{1,0:T(4,128)} %get-tuple-element.14.refs_2_, ...), custom_call_target="tpu_custom_call" | custom-call | tf_op jit(solution)/shard_map/pallas_call | solution.py:523

commit v3 on v2

--- a/solution.py
+++ b/solution.py
@@ -47,7 +47,7 @@
     own_ref, other_ref, dq_ref, dk_ref, dv_ref, sendsel_ref,
     idx_send, idx_got, idx_all, send_buf, got, grad_ref, reply_buf, returned,
     load_sem, store_sem, x_send, x_recv, do_send, do_recv, idx_ssem, idx_rsem, idxf_ssem, idxf_rsem,
-    row_ssem, row_rsem, fwd_ssem, fwd_rsem, rep_ssem, rep_rsem,
+    row_ssem, row_rsem, fwd_ssem, fwd_rsem, rep_ssem, rep_rsem, rel_ssem, xr_send, dor_send,
 ):
     pos = lax.axis_index("seq")
     me = lax.axis_index("table")
@@ -58,12 +58,25 @@
     history_scale = 1.0 / math.sqrt(tokens * seq_count)
     temper = 1.0 / math.sqrt(head_size)
     turn = 1 - 2 * (pos % 2)
+    side = math.isqrt(seq_count)
+    my_row, my_col = pos // side, pos % side
+
+    def row_peer(i):
+        return my_row * side + lax.rem(my_col + i, side)
+
+    def col_peer(i):
+        return lax.rem(my_row + i, side) * side + my_col
 
     def seq_peer(r):
         return lax.rem(pos + turn * r + seq_count, seq_count)
 
     def table_peer(r):
-        return lax.rem(me + r, owner_count)
+        peer, bit = 0, 1
+        while bit < owner_count:
+            mine, other = (me // bit) % 2, (r // bit) % 2
+            peer = peer + bit * (mine + other - 2 * mine * other)
+            bit *= 2
+        return peer
 
     def rows_of(owner):
         return pl.ds(pl.multiple_of(owner * capacity, capacity), capacity)
@@ -115,20 +128,67 @@
     pl.semaphore_wait(barrier, seq_count + owner_count - 2)
 
     def x_copy(peer):
-        return to_seq(x_hbm, x_all.at[pos], x_send.at[peer], x_recv.at[pos], peer)
+        return to_seq(x_ref, x_all.at[pos], x_send.at[peer], x_recv.at[pos], peer)
 
     def do_copy(peer):
-        return to_seq(do_hbm, do_all.at[pos], do_send.at[peer], do_recv.at[pos], peer)
-
-    def send_block(r):
-        peer = seq_peer(r)
-        x_copy(peer).start()
-
-        @pl.when(peer < pos)
+        return to_seq(do_ref, do_all.at[pos], do_send.at[peer], do_recv.at[pos], peer)
+
+    for load in loads[3:5]:
+        load.wait()
+
+    def send_x(i):
+        x_copy(row_peer(i)).start()
+        x_copy(col_peer(i)).start()
+
+    def each_do(act):
+        def one(i):
+            for peer in (row_peer(i), col_peer(i)):
+                @pl.when(peer < pos)
+                def _():
+                    act(do_copy(peer))
+
+        each(1, side, one)
+
+    each(1, side, send_x)
+    each_do(lambda copy: copy.start())
+
+    def x_relay(block, peer):
+        return to_seq(
+            x_all.at[block], x_all.at[block], xr_send.at[block], x_recv.at[block], peer
+        )
+
+    def do_relay(block, peer):
+        return to_seq(
+            do_all.at[block], do_all.at[block], dor_send.at[block], do_recv.at[block], peer
+        )
+
+    def relay_x(i):
+        for block, to_peer, first in ((row_peer(i), col_peer, 0), (col_peer(i), row_peer, 1)):
+            x_relay(block, block).wait_recv()
+
+            @pl.when((block // side + block % side) % 2 == first)
+            def _():
+                each(1, side, lambda k: x_relay(block, to_peer(k)).start())
+
+    def relay_do(i):
+        block = col_peer(i)
+
+        @pl.when(block > pos)
         def _():
-            do_copy(peer).start()
-
-    each(1, seq_count, send_block)
+            do_relay(block, block).wait_recv()
+            each(1, side, lambda k: do_relay(block, row_peer(k)).start())
+
+    def end_relays(i):
+        for block, to_peer, first in ((row_peer(i), col_peer, 0), (col_peer(i), row_peer, 1)):
+            @pl.when((block // side + block % side) % 2 == first)
+            def _():
+                each(1, side, lambda k: x_relay(block, to_peer(k)).wait_send())
+
+        below = col_peer(i)
+
+        @pl.when(below > pos)
+        def _():
+            each(1, side, lambda k: do_relay(below, row_peer(k)).wait_send())
 
     eye = iota((LANES, LANES), 0) == iota((LANES, LANES), 1)
 
@@ -190,7 +250,7 @@
     each(1, owner_count, lambda r: idx_copy(table_peer(r)).start())
     idx_got[me] = idx_send[me]
 
-    for load in loads[3:6]:
+    for load in loads[5:6]:
         load.wait()
     x_all[pos] = x_ref[...]
     do_all[pos] = do_ref[...]
@@ -228,11 +288,11 @@
     def block_step(r):
         block = seq_peer(r)
 
-        @pl.when(r > 0)
+        in_row, in_col = block // side == my_row, block % side == my_col
+
+        @pl.when(jnp.logical_not(in_row | in_col))
         def _():
-            to_seq(
-                x_all.at[block], x_all.at[block], x_send.at[block], x_recv.at[block], block
-            ).wait_recv()
+            x_relay(block, block).wait_recv()
 
         @pl.when(block <= pos)
         def _():
@@ -260,9 +320,10 @@
         def _():
             @pl.when(block > pos)
             def _():
-                to_seq(
-                    do_all.at[block], do_all.at[block], do_send.at[block], do_recv.at[block], block
-                ).wait_recv()
+                @pl.when(jnp.logical_not(in_col))
+                def _():
+                    do_relay(block, block).wait_recv()
+
                 other_ref[:, :features] = dot(x_all[block], proj_ref[:, :features]).astype(BF16)
 
             @pl.when(block == pos)
@@ -286,7 +347,10 @@
                 dk_ref[:, cols] += dot(score_grad, queries)
                 dv_ref[:, cols] += dot(weights, grads)
 
-    each(0, seq_count, block_step)
+    block_step(0)
+    each(1, side, relay_x)
+    each(1, side, relay_do)
+    each(1, seq_count, block_step)
 
     def take_index(r):
         peer = table_peer(r)
@@ -314,28 +378,51 @@
             row_ssem.at[peer], row_rsem.at[me], peer,
         )
 
-    each(1, owner_count, lambda r: row_copy(table_peer(r)).start())
+    each(1, owner_count, lambda r: row_copy(table_peer(owner_count - r)).start())
     got[pos, rows_of(me)] = send_buf[rows_of(me)]
 
+    def chunk(block, source, ssem, peer):
+        part = got.at[block, rows_of(source)]
+        return to_seq(part, part, ssem, fwd_rsem.at[block, source], peer)
+
     def forward(source):
-        def one(r):
-            peer = seq_peer(r)
-            to_seq(
-                got.at[pos, rows_of(source)], got.at[pos, rows_of(source)],
-                fwd_ssem.at[peer], fwd_rsem.at[pos], peer,
-            ).start()
-
-        each(1, seq_count, one)
+        def one(i):
+            chunk(pos, source, fwd_ssem.at[row_peer(i)], row_peer(i)).start()
+            chunk(pos, source, fwd_ssem.at[col_peer(i)], col_peer(i)).start()
+
+        each(1, side, one)
+
+    def pass_chunk(source):
+        def along(from_peer, to_peer):
+            def one(i):
+                block = from_peer(i)
+                chunk(block, source, rel_ssem.at[block], block).wait_recv()
+                each(
+                    1, side,
+                    lambda k: chunk(block, source, rel_ssem.at[block], to_peer(k)).start(),
+                )
+
+            each(1, side, one)
+
+        @pl.when(source % 2 == 0)
+        def _():
+            along(row_peer, col_peer)
+
+        @pl.when(source % 2 == 1)
+        def _():
+            along(col_peer, row_peer)
 
     forward(me)
 
     def relay(r):
-        source = lax.rem(me - r + owner_count, owner_count)
+        source = table_peer(r)
         part = got.at[pos, rows_of(source)]
         to_table(part, part, row_ssem.at[source], row_rsem.at[source], source).wait_recv()
         forward(source)
+        pass_chunk(table_peer(r - 1))
 
     each(1, owner_count, relay)
+    pass_chunk(table_peer(owner_count - 1))
 
     slab_ids = iota((slab_rows, width), 0).astype(F32) + 1.0
 
@@ -349,9 +436,15 @@
         to_seq(
             idx_all.at[block], idx_all.at[block], idxf_ssem.at[block], idxf_rsem.at[block], block
         ).wait_recv()
-        to_seq(
-            got.at[block], got.at[block], fwd_ssem.at[block], fwd_rsem.at[block], block
-        ).wait_recv()
+        in_row, in_col = block // side == my_row, block % side == my_col
+
+        def await_pair(half):
+            for odd, seen in ((0, in_row), (1, in_col)):
+                @pl.when(jnp.logical_not(seen))
+                def _():
+                    chunk(block, 2 * half + odd, rel_ssem.at[block], block).wait_recv()
+
+        each(0, owner_count // 2, await_pair)
         grad_ref[...] += dot(select(block), got[block])
 
     each(1, seq_count, add_block)
@@ -389,18 +482,23 @@
         store.start()
     returned[rows_of(me)] = reply_buf[rows_of(me)]
 
-    def end_seq(r):
-        peer = seq_peer(r)
-        x_copy(peer).wait_send()
-
-        @pl.when(peer < pos)
-        def _():
-            do_copy(peer).wait_send()
-
-        idxf_copy(peer).wait_send()
-        to_seq(got.at[pos], got.at[pos], fwd_ssem.at[peer], fwd_rsem.at[pos], peer).wait_send()
-
-    each(1, seq_count, end_seq)
+    each(1, seq_count, lambda r: idxf_copy(seq_peer(r)).wait_send())
+    each_do(lambda copy: copy.wait_send())
+
+    def end_seq(i):
+        for peer in (row_peer(i), col_peer(i)):
+            x_copy(peer).wait_send()
+            to_seq(
+                got.at[pos], got.at[pos], fwd_ssem.at[peer], fwd_rsem.at[pos, 0], peer
+            ).wait_send()
+            half = got.at[peer, pl.ds(0, width // 2)]
+            for _ in range(side - 1):
+                to_seq(
+                    half, half, rel_ssem.at[peer], fwd_rsem.at[peer, 0], peer
+                ).wait_send()
+
+    each(1, side, end_seq)
+    each(1, side, end_relays)
 
     def end_table(r):
         peer = table_peer(r)
@@ -420,22 +518,30 @@
 
 
 def pass_on(*refs):
-    sems = refs[-1]
-    half = len(refs) // 2
-    copies = []
-    for source, target in zip(refs[:half], refs[half:-1]):
+    count = len(refs) // 3
+    sources, targets, held = refs[:count], refs[count : 2 * count], refs[2 * count : 3 * count]
+    in_sem, out_sem = refs[3 * count :]
+    loads, stores = [], []
+    for source, target, stage in zip(sources, targets, held):
         rows = source.shape[0]
         pieces = rows // LANES if rows > LANES else 1
         size = rows // pieces
         for piece in range(pieces):
             part = pl.ds(piece * size, size)
-            copies.append(
-                pltpu.make_async_copy(source.at[part], target.at[part], sems.at[len(copies)])
+            number = len(loads)
+            loads.append(
+                pltpu.make_async_copy(source.at[part], stage.at[part], in_sem.at[number])
             )
-    for copy in copies:
-        copy.start()
-    for copy in copies:
-        copy.wait()
+            stores.append(
+                pltpu.make_async_copy(stage.at[part], target.at[part], out_sem.at[number])
+            )
+    for load in loads:
+        load.start()
+    for load, store in zip(loads, stores):
+        load.wait()
+        store.start()
+    for store in stores:
+        store.wait()
 
 
 def body(events_x, proj, out_grad, block_mask, item_ids, owner_of, local_of, table, moment, second):
@@ -501,9 +607,12 @@
             dma((owner_count,)),
             dma((owner_count,)),
             dma((seq_count,)),
-            dma((seq_count,)),
+            dma((seq_count, owner_count)),
             dma((owner_count,)),
             dma((owner_count,)),
+            dma((seq_count,)),
+            dma((seq_count,)),
+            dma((seq_count,)),
         ],
         compiler_params=pltpu.CompilerParams(
             collective_id=0, has_side_effects=True, vmem_limit_bytes=VMEM_BYTES
@@ -525,7 +634,8 @@
         out_shape=tuple(jax.ShapeDtypeStruct(r.shape, r.dtype) for r in results),
         in_specs=[hbm] * 4,
         out_specs=(hbm,) * 4,
-        scratch_shapes=[dma((2 * (slab_rows // LANES) + 2,))],
+        scratch_shapes=[pltpu.VMEM(r.shape, r.dtype) for r in results]
+        + [dma((2 * (slab_rows // LANES) + 2,))] * 2,
         compiler_params=pltpu.CompilerParams(vmem_limit_bytes=VMEM_BYTES),
     )(*results)
     return (new_table, new_moment, new_second.reshape(-1), event_rows[None])

time: 100 us -> 49.6 us (0.50)
  Pallas kernels: 99.2 us -> 48.8 us
    pallas_call x1, Pallas kernels: 52.9 us -> 2.39 us  [body(): pl.pallas_call(pass_on, out_shape=tuple((jax.ShapeDtypeStruct(r.shape, r....]
where the time goes in v3:
time: 49.6 us; the launch traced here: 49.4 us
  Pallas kernels  48.8 us (98%)
  between operations  0.64 us (1%)
    pallas_call x1, Pallas kernels, body(): pl.pallas_call(functools.partial(kernel, seq_count, owner_count, capacity...  46.4 us
    pallas_call x1, Pallas kernels, body(): pl.pallas_call(pass_on, out_shape=tuple((jax.ShapeDtypeStruct(r.shape, r....  2.39 us

profile of v3, /device:TPU:0, one launch (start us, length us, event | category | flops | bytes accessed | tf_op | source)
XLA Modules:
  0.0 49.4 jit_solution(2278132118343162563)
XLA Ops:
  0.6 46.4 %shard_map.129 = (bf16[512,512]{1,0:T(8,128)(2,1)}, f32[512,512]{1,0:T(8,128)}, f32[4,128]{1,0:T(4,128)}, bf16[128,512]{1,0:T(8,128)(2,1)}) custom-call(bf16[128,512]{1,0:T(8,128)(2,1)} %bitcast.7, bf16[512,1536]{1,0:T(8,128)(2,1)} %proj_hbm.1, bf16[128,512]{1,0:T(8,128)(2,1)} %bitcast.8, s32[4,4]{1,0:T(4,128)} %mask_ref.1, s32[1,128]{1,0:T(1,128)} %ids_hbm.1, ...), custom_call_target="tpu_custom_call" | custom-call | tf_op jit(solution)/shard_map/pallas_call | solution.py:557
  47.0 2.4 %shard_map.130 = (bf16[512,512]{1,0:T(8,128)(2,1)}, f32[512,512]{1,0:T(8,128)}, f32[4,128]{1,0:T(4,128)}, bf16[128,512]{1,0:T(8,128)(2,1)}) custom-call(bf16[512,512]{1,0:T(8,128)(2,1)} %get-tuple-element.12.refs_0_, f32[512,512]{1,0:T(8,128)} %get-tuple-element.13.refs_1_, f32[4,128]{1,0:T(4,128)} %get-tuple-element.14.refs_2_, ...), custom_call_target="tpu_custom_call" | custom-call | tf_op jit(solution)/shard_map/pallas_call | solution.py:632

commit v4 on v3

--- a/solution.py
+++ b/solution.py
@@ -34,18 +34,14 @@
     return lax.dot_general(a, b, (((1,), (1,)), ((), ())), preferred_element_type=F32)
 
 
-def dot_tn(a, b):
-    return lax.dot_general(a, b, (((0,), (0,)), ((), ())), preferred_element_type=F32)
-
-
 def kernel(
     seq_count, owner_count, capacity,
     x_hbm, proj_hbm, do_hbm, mask_ref, ids_hbm, owner_hbm, local_hbm, table_hbm, moment_hbm, second_hbm,
-    ntab_hbm, nmom_hbm, nsec_hbm, event_hbm,
-    x_ref, do_ref, ids_ref, owner_ref, local_ref, second_ref, nsec_ref, event_ref,
+    ntab_hbm, nmom_hbm, nsec_hbm, recvsel_hbm, returned,
+    x_ref, do_ref, ids_ref, owner_ref, local_ref, second_ref, nsec_ref, recvsel_ref, select_ref, replysel_ref,
     x_all, do_all, proj_ref, table_ref, moment_ref, ntab_ref, nmom_ref,
     own_ref, other_ref, dq_ref, dk_ref, dv_ref, sendsel_ref,
-    idx_send, idx_got, idx_all, send_buf, got, grad_ref, reply_buf, returned,
+    idx_send, idx_got, idx_all, send_buf, got, grad_ref, reply_buf,
     load_sem, store_sem, x_send, x_recv, do_send, do_recv, idx_ssem, idx_rsem, idxf_ssem, idxf_rsem,
     row_ssem, row_rsem, fwd_ssem, fwd_rsem, rep_ssem, rep_rsem, rel_ssem, xr_send, dor_send,
 ):
@@ -231,6 +227,12 @@
     sendsel_ref[...] = jnp.where(
         iota((width, tokens), 0).astype(F32) == target_row, 1.0, 0.0
     ).astype(BF16)
+    target_col = owner_col * capacity + slot_col
+    recvsel_ref[...] = jnp.where(
+        iota((tokens, width), 1).astype(F32) == target_col, 1.0, 0.0
+    ).astype(BF16)
+    recvsel_store = pltpu.make_async_copy(recvsel_ref, recvsel_hbm, store_sem.at[3])
+    recvsel_store.start()
     lane_col = slot_col + (me * capacity).astype(F32)
     marks = jnp.where(iota((tokens, width), 1).astype(F32) == lane_col, local_col + 1.0, 0.0)
 
@@ -348,9 +350,6 @@
                 dv_ref[:, cols] += dot(weights, grads)
 
     block_step(0)
-    each(1, side, relay_x)
-    each(1, side, relay_do)
-    each(1, seq_count, block_step)
 
     def take_index(r):
         peer = table_peer(r)
@@ -365,6 +364,34 @@
         return to_seq(idx_all.at[pos], idx_all.at[pos], idxf_ssem.at[peer], idxf_rsem.at[pos], peer)
 
     each(1, seq_count, lambda r: idxf_copy(seq_peer(r)).start())
+
+    each(1, side, relay_x)
+
+    slab_ids = iota((slab_rows, width), 0).astype(F32) + 1.0
+
+    def select(block):
+        select_ref[block] = jnp.where(
+            slab_ids == idx_all[block][0:1, :], 1.0, 0.0
+        ).astype(BF16)
+
+    select(pos)
+    slab_lanes = iota((LANES, slab_rows), 1).astype(F32) + 1.0
+    for c in range(width // LANES):
+        lanes = slice(c * LANES, (c + 1) * LANES)
+        replysel_ref[lanes, :] = jnp.where(
+            slab_lanes == to_col(idx_all[pos][0:1, lanes]), 1.0, 0.0
+        ).astype(BF16)
+
+    def select_other(r):
+        block = seq_peer(r)
+        to_seq(
+            idx_all.at[block], idx_all.at[block], idxf_ssem.at[block], idxf_rsem.at[block], block
+        ).wait_recv()
+        select(block)
+
+    each(1, seq_count, select_other)
+    each(1, side, relay_do)
+    each(1, seq_count, block_step)
 
     stacked = jnp.concatenate(
         [dq_ref[...].astype(BF16), dk_ref[...].astype(BF16), dv_ref[...].astype(BF16)], axis=1
@@ -424,18 +451,10 @@
     each(1, owner_count, relay)
     pass_chunk(table_peer(owner_count - 1))
 
-    slab_ids = iota((slab_rows, width), 0).astype(F32) + 1.0
-
-    def select(block):
-        return jnp.where(slab_ids == idx_all[block][0:1, :], 1.0, 0.0).astype(BF16)
-
-    grad_ref[...] = dot(select(pos), got[pos])
+    grad_ref[...] = dot(select_ref[pos], got[pos])
 
     def add_block(r):
         block = seq_peer(r)
-        to_seq(
-            idx_all.at[block], idx_all.at[block], idxf_ssem.at[block], idxf_rsem.at[block], block
-        ).wait_recv()
         in_row, in_col = block // side == my_row, block % side == my_col
 
         def await_pair(half):
@@ -445,7 +464,7 @@
                     chunk(block, 2 * half + odd, rel_ssem.at[block], block).wait_recv()
 
         each(0, owner_count // 2, await_pair)
-        grad_ref[...] += dot(select(block), got[block])
+        grad_ref[...] += dot(select_ref[block], got[block])
 
     each(1, seq_count, add_block)
 
@@ -464,7 +483,7 @@
         factor = step_rate / (jnp.sqrt(new_second) + epsilon)
         ntab_ref[rows, :] = (table_ref[rows, :].astype(F32) - new_moment * factor).astype(BF16)
 
-    reply_buf[...] = dot_tn(select(pos), ntab_ref[...]).astype(BF16)
+    reply_buf[...] = dot(replysel_ref[...], ntab_ref[...]).astype(BF16)
 
     def reply_copy(peer):
         return to_table(
@@ -477,10 +496,12 @@
         pltpu.make_async_copy(nmom_ref, nmom_hbm, store_sem.at[0]),
         pltpu.make_async_copy(ntab_ref, ntab_hbm, store_sem.at[1]),
         pltpu.make_async_copy(nsec_ref, nsec_hbm, store_sem.at[2]),
+        pltpu.make_async_copy(
+            reply_buf.at[rows_of(me)], returned.at[rows_of(me)], store_sem.at[4]
+        ),
     ]
     for store in stores:
         store.start()
-    returned[rows_of(me)] = reply_buf[rows_of(me)]
 
     each(1, seq_count, lambda r: idxf_copy(seq_peer(r)).wait_send())
     each_do(lambda copy: copy.wait_send())
@@ -508,21 +529,27 @@
         to_table(part, part, rep_ssem.at[peer], rep_rsem.at[peer], peer).wait_recv()
 
     each(1, owner_count, end_table)
-    event_ref[...] = dot_tn(sendsel_ref[...], returned[...]).astype(BF16)
-    last = pltpu.make_async_copy(event_ref, event_hbm, store_sem.at[3])
-    last.start()
     each(1, owner_count, lambda r: reply_copy(table_peer(r)).wait_send())
     for store in stores:
         store.wait()
-    last.wait()
-
-
-def pass_on(*refs):
-    count = len(refs) // 3
-    sources, targets, held = refs[:count], refs[count : 2 * count], refs[2 * count : 3 * count]
-    in_sem, out_sem = refs[3 * count :]
+    recvsel_store.wait()
+
+
+def finish(
+    ntab_hbm, nmom_hbm, nsec_hbm, recvsel_hbm, returned_hbm,
+    ntab_out, nmom_out, nsec_out, event_out,
+    ntab_ref, nmom_ref, nsec_ref, recvsel_ref, returned_ref, event_ref, in_sem, out_sem, event_sem,
+):
+    waits = [
+        pltpu.make_async_copy(returned_hbm, returned_ref, event_sem.at[0]),
+        pltpu.make_async_copy(recvsel_hbm, recvsel_ref, event_sem.at[1]),
+    ]
     loads, stores = [], []
-    for source, target, stage in zip(sources, targets, held):
+    for source, target, stage in (
+        (nmom_hbm, nmom_out, nmom_ref),
+        (ntab_hbm, ntab_out, ntab_ref),
+        (nsec_hbm, nsec_out, nsec_ref),
+    ):
         rows = source.shape[0]
         pieces = rows // LANES if rows > LANES else 1
         size = rows // pieces
@@ -535,8 +562,13 @@
             stores.append(
                 pltpu.make_async_copy(stage.at[part], target.at[part], out_sem.at[number])
             )
-    for load in loads:
+    for load in waits + loads:
         load.start()
+    for load in waits:
+        load.wait()
+    event_ref[...] = dot(recvsel_ref[...], returned_ref[...]).astype(BF16)
+    stores.append(pltpu.make_async_copy(event_ref, event_out, event_sem.at[2]))
+    stores[-1].start()
     for load, store in zip(loads, stores):
         load.wait()
         store.start()
@@ -560,10 +592,11 @@
             jax.ShapeDtypeStruct((slab_rows, features), BF16),
             jax.ShapeDtypeStruct((slab_rows, features), F32),
             jax.ShapeDtypeStruct((slab_rows // LANES, LANES), F32),
-            jax.ShapeDtypeStruct((tokens, features), BF16),
+            jax.ShapeDtypeStruct((tokens, width), BF16),
+            jax.ShapeDtypeStruct((width, features), BF16),
         ),
         in_specs=[hbm, hbm, hbm, smem] + [hbm] * 6,
-        out_specs=(hbm,) * 4,
+        out_specs=(hbm,) * 5,
         scratch_shapes=[
             pltpu.VMEM((tokens, features), BF16),
             pltpu.VMEM((tokens, features), BF16),
@@ -572,7 +605,9 @@
             pltpu.VMEM((owner_of.shape[0] // LANES, LANES), jnp.int32),
             pltpu.VMEM((slab_rows // LANES, LANES), F32),
             pltpu.VMEM((slab_rows // LANES, LANES), F32),
-            pltpu.VMEM((tokens, features), BF16),
+            pltpu.VMEM((tokens, width), BF16),
+            pltpu.VMEM((seq_count, slab_rows, width), BF16),
+            pltpu.VMEM((width, slab_rows), BF16),
             pltpu.VMEM((seq_count, tokens, features), BF16),
             pltpu.VMEM((seq_count, tokens, features), BF16),
             pltpu.VMEM(proj.shape, BF16),
@@ -593,9 +628,8 @@
             pltpu.VMEM((seq_count, width, features), BF16),
             pltpu.VMEM((slab_rows, features), F32),
             pltpu.VMEM((width, features), BF16),
-            pltpu.VMEM((width, features), BF16),
             dma((9,)),
-            dma((4,)),
+            dma((5,)),
             dma((seq_count,)),
             dma((seq_count,)),
             dma((seq_count,)),
@@ -629,13 +663,16 @@
         moment,
         second.reshape(-1, LANES),
     )
+    outs = [(r.shape, r.dtype) for r in results]
+    events = ((tokens, features), BF16)
     new_table, new_moment, new_second, event_rows = pl.pallas_call(
-        pass_on,
-        out_shape=tuple(jax.ShapeDtypeStruct(r.shape, r.dtype) for r in results),
-        in_specs=[hbm] * 4,
+        finish,
+        out_shape=tuple(jax.ShapeDtypeStruct(*o) for o in outs[:3] + [events]),
+        in_specs=[hbm] * 5,
         out_specs=(hbm,) * 4,
-        scratch_shapes=[pltpu.VMEM(r.shape, r.dtype) for r in results]
-        + [dma((2 * (slab_rows // LANES) + 2,))] * 2,
+        scratch_shapes=[pltpu.VMEM(*o) for o in outs + [events]]
+        + [dma((2 * (slab_rows // LANES) + 1,))] * 2
+        + [dma((3,))],
         compiler_params=pltpu.CompilerParams(vmem_limit_bytes=VMEM_BYTES),
     )(*results)
     return (new_table, new_moment, new_second.reshape(-1), event_rows[None])

time: 49.6 us -> 50.2 us (1.012)
  Pallas kernels: 48.8 us -> 49.4 us
    pallas_call x1, Pallas kernels: 2.39 us -> 2.94 us  [body(): pl.pallas_call(finish, out_shape=tuple((jax.ShapeDtypeStruct(*o) for o in...]
where the time goes in v4:
time: 50.2 us; the launch traced here: 50 us
  Pallas kernels  49.4 us (98%)
  between operations  0.64 us (1%)
    pallas_call x1, Pallas kernels, body(): pl.pallas_call(functools.partial(kernel, seq_count, owner_count, capacity...  46.4 us
    pallas_call x1, Pallas kernels, body(): pl.pallas_call(finish, out_shape=tuple((jax.ShapeDtypeStruct(*o) for o in...  2.94 us

profile of v4, /device:TPU:0, one launch (start us, length us, event | category | flops | bytes accessed | tf_op | source)
XLA Modules:
  0.0 50.0 jit_solution(12481723977335709549)
XLA Ops:
  0.6 46.4 %shard_map.129 = (bf16[512,512]{1,0:T(8,128)(2,1)}, f32[512,512]{1,0:T(8,128)}, f32[4,128]{1,0:T(4,128)}, bf16[128,256]{1,0:T(8,128)(2,1)}, bf16[256,512]{1,0:T(8,128)(2,1)}) custom-call(bf16[128,512]{1,0:T(8,128)(2,1)} %bitcast.7, bf16[512,1536]{1,0:T(8,128)(2,1)} %proj_hbm.1, bf16[128,512]{1,0:T(8,128)(2,1)} %bitcast.8, s32[4,4]{1,0:T(4,128)} %mask_ref.1, ...), custom_call_target="tpu_custom_call" | custom-call | tf_op jit(solution)/shard_map/pallas_call | solution.py:589
  47.1 2.9 %shard_map.130 = (bf16[512,512]{1,0:T(8,128)(2,1)}, f32[512,512]{1,0:T(8,128)}, f32[4,128]{1,0:T(4,128)}, bf16[128,512]{1,0:T(8,128)(2,1)}) custom-call(bf16[512,512]{1,0:T(8,128)(2,1)} %get-tuple-element.13.ntab_hbm, f32[512,512]{1,0:T(8,128)} %get-tuple-element.14.nmom_hbm, f32[4,128]{1,0:T(4,128)} %get-tuple-element.15.nsec_hbm, ...), custom_call_target="tpu_custom_call" | custom-call | tf_op jit(solution)/shard_map/pallas_call | solution.py:668

commit v5 on v3

--- a/solution.py
+++ b/solution.py
@@ -34,20 +34,16 @@
     return lax.dot_general(a, b, (((1,), (1,)), ((), ())), preferred_element_type=F32)
 
 
-def dot_tn(a, b):
-    return lax.dot_general(a, b, (((0,), (0,)), ((), ())), preferred_element_type=F32)
-
-
 def kernel(
     seq_count, owner_count, capacity,
     x_hbm, proj_hbm, do_hbm, mask_ref, ids_hbm, owner_hbm, local_hbm, table_hbm, moment_hbm, second_hbm,
     ntab_hbm, nmom_hbm, nsec_hbm, event_hbm,
-    x_ref, do_ref, ids_ref, owner_ref, local_ref, second_ref, nsec_ref, event_ref,
+    x_ref, do_ref, ids_ref, owner_ref, local_ref, second_ref, nsec_ref, event_ref, returned, recvsel_ref, select_ref, replysel_ref,
     x_all, do_all, proj_ref, table_ref, moment_ref, ntab_ref, nmom_ref,
     own_ref, other_ref, dq_ref, dk_ref, dv_ref, sendsel_ref,
-    idx_send, idx_got, idx_all, send_buf, got, grad_ref, reply_buf, returned,
+    idx_send, idx_got, idx_all, send_buf, got, grad_ref, reply_buf,
     load_sem, store_sem, x_send, x_recv, do_send, do_recv, idx_ssem, idx_rsem, idxf_ssem, idxf_rsem,
-    row_ssem, row_rsem, fwd_ssem, fwd_rsem, rep_ssem, rep_rsem, rel_ssem, xr_send, dor_send,
+    row_ssem, row_rsem, fwd_ssem, fwd_rsem, rep_ssem, rep_rsem, rel_ssem, xr_send, diag_ssem,
 ):
     pos = lax.axis_index("seq")
     me = lax.axis_index("table")
@@ -141,13 +137,14 @@
         x_copy(col_peer(i)).start()
 
     def each_do(act):
-        def one(i):
-            for peer in (row_peer(i), col_peer(i)):
-                @pl.when(peer < pos)
-                def _():
-                    act(do_copy(peer))
-
-        each(1, side, one)
+        def one(r):
+            peer = seq_peer(r)
+
+            @pl.when(peer < pos)
+            def _():
+                act(do_copy(peer))
+
+        each(1, seq_count, one)
 
     each(1, side, send_x)
     each_do(lambda copy: copy.start())
@@ -157,38 +154,19 @@
             x_all.at[block], x_all.at[block], xr_send.at[block], x_recv.at[block], peer
         )
 
-    def do_relay(block, peer):
-        return to_seq(
-            do_all.at[block], do_all.at[block], dor_send.at[block], do_recv.at[block], peer
-        )
-
     def relay_x(i):
         for block, to_peer, first in ((row_peer(i), col_peer, 0), (col_peer(i), row_peer, 1)):
             x_relay(block, block).wait_recv()
 
-            @pl.when((block // side + block % side) % 2 == first)
+            @pl.when((block // side) % 2 == first)
             def _():
                 each(1, side, lambda k: x_relay(block, to_peer(k)).start())
-
-    def relay_do(i):
-        block = col_peer(i)
-
-        @pl.when(block > pos)
-        def _():
-            do_relay(block, block).wait_recv()
-            each(1, side, lambda k: do_relay(block, row_peer(k)).start())
 
     def end_relays(i):
         for block, to_peer, first in ((row_peer(i), col_peer, 0), (col_peer(i), row_peer, 1)):
-            @pl.when((block // side + block % side) % 2 == first)
+            @pl.when((block // side) % 2 == first)
             def _():
                 each(1, side, lambda k: x_relay(block, to_peer(k)).wait_send())
-
-        below = col_peer(i)
-
-        @pl.when(below > pos)
-        def _():
-            each(1, side, lambda k: do_relay(below, row_peer(k)).wait_send())
 
     eye = iota((LANES, LANES), 0) == iota((LANES, LANES), 1)
 
@@ -231,6 +209,10 @@
     sendsel_ref[...] = jnp.where(
         iota((width, tokens), 0).astype(F32) == target_row, 1.0, 0.0
     ).astype(BF16)
+    target_col = owner_col * capacity + slot_col
+    recvsel_ref[...] = jnp.where(
+        iota((tokens, width), 1).astype(F32) == target_col, 1.0, 0.0
+    ).astype(BF16)
     lane_col = slot_col + (me * capacity).astype(F32)
     marks = jnp.where(iota((tokens, width), 1).astype(F32) == lane_col, local_col + 1.0, 0.0)
 
@@ -320,11 +302,10 @@
         def _():
             @pl.when(block > pos)
             def _():
-                @pl.when(jnp.logical_not(in_col))
-                def _():
-                    do_relay(block, block).wait_recv()
-
                 other_ref[:, :features] = dot(x_all[block], proj_ref[:, :features]).astype(BF16)
+                to_seq(
+                    do_all.at[block], do_all.at[block], do_send.at[block], do_recv.at[block], block
+                ).wait_recv()
 
             @pl.when(block == pos)
             def _():
@@ -348,9 +329,6 @@
                 dv_ref[:, cols] += dot(weights, grads)
 
     block_step(0)
-    each(1, side, relay_x)
-    each(1, side, relay_do)
-    each(1, seq_count, block_step)
 
     def take_index(r):
         peer = table_peer(r)
@@ -366,6 +344,33 @@
 
     each(1, seq_count, lambda r: idxf_copy(seq_peer(r)).start())
 
+    each(1, side, relay_x)
+
+    slab_ids = iota((slab_rows, width), 0).astype(F32) + 1.0
+
+    def select(block):
+        select_ref[block] = jnp.where(
+            slab_ids == idx_all[block][0:1, :], 1.0, 0.0
+        ).astype(BF16)
+
+    select(pos)
+    slab_lanes = iota((LANES, slab_rows), 1).astype(F32) + 1.0
+    for c in range(width // LANES):
+        lanes = slice(c * LANES, (c + 1) * LANES)
+        replysel_ref[lanes, :] = jnp.where(
+            slab_lanes == to_col(idx_all[pos][0:1, lanes]), 1.0, 0.0
+        ).astype(BF16)
+
+    def select_other(r):
+        block = seq_peer(r)
+        to_seq(
+            idx_all.at[block], idx_all.at[block], idxf_ssem.at[block], idxf_rsem.at[block], block
+        ).wait_recv()
+        select(block)
+
+    each(1, seq_count, select_other)
+    each(1, seq_count, block_step)
+
     stacked = jnp.concatenate(
         [dq_ref[...].astype(BF16), dk_ref[...].astype(BF16), dv_ref[...].astype(BF16)], axis=1
     )
@@ -391,6 +396,22 @@
             chunk(pos, source, fwd_ssem.at[col_peer(i)], col_peer(i)).start()
 
         each(1, side, one)
+
+    near = owner_count // 2
+
+    def each_diag(act):
+        def one(r):
+            peer = seq_peer(r)
+
+            @pl.when(jnp.logical_not((peer // side == my_row) | (peer % side == my_col)))
+            def _():
+                act(peer)
+
+        each(1, seq_count, one)
+
+    def forward_far(source):
+        forward(source)
+        each_diag(lambda peer: chunk(pos, source, diag_ssem.at[peer], peer).start())
 
     def pass_chunk(source):
         def along(from_peer, to_peer):
@@ -414,38 +435,36 @@
 
     forward(me)
 
-    def relay(r):
+    def take_chunk(r):
         source = table_peer(r)
         part = got.at[pos, rows_of(source)]
         to_table(part, part, row_ssem.at[source], row_rsem.at[source], source).wait_recv()
-        forward(source)
+        return source
+
+    def relay(r):
+        forward(take_chunk(r))
         pass_chunk(table_peer(r - 1))
 
-    each(1, owner_count, relay)
-    pass_chunk(table_peer(owner_count - 1))
-
-    slab_ids = iota((slab_rows, width), 0).astype(F32) + 1.0
-
-    def select(block):
-        return jnp.where(slab_ids == idx_all[block][0:1, :], 1.0, 0.0).astype(BF16)
-
-    grad_ref[...] = dot(select(pos), got[pos])
+    each(1, near, relay)
+    pass_chunk(table_peer(near - 1))
+    each(near, owner_count, lambda r: forward_far(take_chunk(r)))
+
+    grad_ref[...] = dot(select_ref[pos], got[pos])
 
     def add_block(r):
         block = seq_peer(r)
-        to_seq(
-            idx_all.at[block], idx_all.at[block], idxf_ssem.at[block], idxf_rsem.at[block], block
-        ).wait_recv()
         in_row, in_col = block // side == my_row, block % side == my_col
 
-        def await_pair(half):
-            for odd, seen in ((0, in_row), (1, in_col)):
-                @pl.when(jnp.logical_not(seen))
-                def _():
-                    chunk(block, 2 * half + odd, rel_ssem.at[block], block).wait_recv()
-
-        each(0, owner_count // 2, await_pair)
-        grad_ref[...] += dot(select(block), got[block])
+        def await_chunk(r):
+            source = table_peer(r)
+            passed = (in_row & (source % 2 == 0)) | (in_col & (source % 2 == 1))
+
+            @pl.when(jnp.logical_not(passed & (r < near)))
+            def _():
+                chunk(block, source, rel_ssem.at[block], block).wait_recv()
+
+        each(0, owner_count, await_chunk)
+        grad_ref[...] += dot(select_ref[block], got[block])
 
     each(1, seq_count, add_block)
 
@@ -464,7 +483,7 @@
         factor = step_rate / (jnp.sqrt(new_second) + epsilon)
         ntab_ref[rows, :] = (table_ref[rows, :].astype(F32) - new_moment * factor).astype(BF16)
 
-    reply_buf[...] = dot_tn(select(pos), ntab_ref[...]).astype(BF16)
+    reply_buf[...] = dot(replysel_ref[...], ntab_ref[...]).astype(BF16)
 
     def reply_copy(peer):
         return to_table(
@@ -491,13 +510,19 @@
             to_seq(
                 got.at[pos], got.at[pos], fwd_ssem.at[peer], fwd_rsem.at[pos, 0], peer
             ).wait_send()
-            half = got.at[peer, pl.ds(0, width // 2)]
+            half = got.at[peer, pl.ds(0, width // 4)]
             for _ in range(side - 1):
                 to_seq(
                     half, half, rel_ssem.at[peer], fwd_rsem.at[peer, 0], peer
                 ).wait_send()
 
     each(1, side, end_seq)
+    far = got.at[pos, pl.ds(0, width // 2)]
+    each_diag(
+        lambda peer: to_seq(
+            far, far, diag_ssem.at[peer], fwd_rsem.at[pos, 0], peer
+        ).wait_send()
+    )
     each(1, side, end_relays)
 
     def end_table(r):
@@ -508,7 +533,7 @@
         to_table(part, part, rep_ssem.at[peer], rep_rsem.at[peer], peer).wait_recv()
 
     each(1, owner_count, end_table)
-    event_ref[...] = dot_tn(sendsel_ref[...], returned[...]).astype(BF16)
+    event_ref[...] = dot(recvsel_ref[...], returned[...]).astype(BF16)
     last = pltpu.make_async_copy(event_ref, event_hbm, store_sem.at[3])
     last.start()
     each(1, owner_count, lambda r: reply_copy(table_peer(r)).wait_send())
@@ -573,6 +598,10 @@
             pltpu.VMEM((slab_rows // LANES, LANES), F32),
             pltpu.VMEM((slab_rows // LANES, LANES), F32),
             pltpu.VMEM((tokens, features), BF16),
+            pltpu.VMEM((width, features), BF16),
+            pltpu.VMEM((tokens, width), BF16),
+            pltpu.VMEM((seq_count, slab_rows, width), BF16),
+            pltpu.VMEM((width, slab_rows), BF16),
             pltpu.VMEM((seq_count, tokens, features), BF16),
             pltpu.VMEM((seq_count, tokens, features), BF16),
             pltpu.VMEM(proj.shape, BF16),
@@ -592,7 +621,6 @@
             pltpu.VMEM((width, features), BF16),
             pltpu.VMEM((seq_count, width, features), BF16),
             pltpu.VMEM((slab_rows, features), F32),
-            pltpu.VMEM((width, features), BF16),
             pltpu.VMEM((width, features), BF16),
             dma((9,)),
             dma((4,)),

time: 49.6 us -> 48.7 us (0.982)
  Pallas kernels: 48.8 us -> 47.8 us
    pallas_call x1, Pallas kernels: 46.4 us -> 45.4 us  [body(): pl.pallas_call(functools.partial(kernel, seq_count, owner_count, capacity...]
where the time goes in v5:
time: 48.7 us; the launch traced here: 48.4 us
  Pallas kernels  47.8 us (98%)
  between operations  0.64 us (1%)
    pallas_call x1, Pallas kernels, body(): pl.pallas_call(functools.partial(kernel, seq_count, owner_count, capacity...  45.4 us
    pallas_call x1, Pallas kernels, body(): pl.pallas_call(pass_on, out_shape=tuple((jax.ShapeDtypeStruct(r.shape, r....  2.39 us

profile of v5, /device:TPU:0, one launch (start us, length us, event | category | flops | bytes accessed | tf_op | source)
XLA Modules:
  0.0 48.4 jit_solution(14470857444953631469)
XLA Ops:
  0.6 45.4 %shard_map.129 = (bf16[512,512]{1,0:T(8,128)(2,1)}, f32[512,512]{1,0:T(8,128)}, f32[4,128]{1,0:T(4,128)}, bf16[128,512]{1,0:T(8,128)(2,1)}) custom-call(bf16[128,512]{1,0:T(8,128)(2,1)} %bitcast.7, bf16[512,1536]{1,0:T(8,128)(2,1)} %proj_hbm.1, bf16[128,512]{1,0:T(8,128)(2,1)} %bitcast.8, s32[4,4]{1,0:T(4,128)} %mask_ref.1, s32[1,128]{1,0:T(1,128)} %ids_hbm.1, ...), custom_call_target="tpu_custom_call" | custom-call | tf_op jit(solution)/shard_map/pallas_call | solution.py:582
  46.0 2.4 %shard_map.130 = (bf16[512,512]{1,0:T(8,128)(2,1)}, f32[512,512]{1,0:T(8,128)}, f32[4,128]{1,0:T(4,128)}, bf16[128,512]{1,0:T(8,128)(2,1)}) custom-call(bf16[512,512]{1,0:T(8,128)(2,1)} %get-tuple-element.12.refs_0_, f32[512,512]{1,0:T(8,128)} %get-tuple-element.13.refs_1_, f32[4,128]{1,0:T(4,128)} %get-tuple-element.14.refs_2_, ...), custom_call_target="tpu_custom_call" | custom-call | tf_op jit(solution)/shard_map/pallas_call | solution.py:660

commit v6 on v5

--- a/solution.py
+++ b/solution.py
@@ -40,7 +40,7 @@
     ntab_hbm, nmom_hbm, nsec_hbm, event_hbm,
     x_ref, do_ref, ids_ref, owner_ref, local_ref, second_ref, nsec_ref, event_ref, returned, recvsel_ref, select_ref, replysel_ref,
     x_all, do_all, proj_ref, table_ref, moment_ref, ntab_ref, nmom_ref,
-    own_ref, other_ref, dq_ref, dk_ref, dv_ref, sendsel_ref,
+    own_ref, scaled_ref, scaled_do_ref, other_ref, dq_ref, dk_ref, dv_ref, sendsel_ref,
     idx_send, idx_got, idx_all, send_buf, got, grad_ref, reply_buf,
     load_sem, store_sem, x_send, x_recv, do_send, do_recv, idx_ssem, idx_rsem, idxf_ssem, idxf_rsem,
     row_ssem, row_rsem, fwd_ssem, fwd_rsem, rep_ssem, rep_rsem, rel_ssem, xr_send, diag_ssem,
@@ -236,10 +236,11 @@
         load.wait()
     x_all[pos] = x_ref[...]
     do_all[pos] = do_ref[...]
-    own_ref[...] = dot(x_ref[...], proj_ref[...]).astype(BF16)
-    dq_ref[...] = jnp.zeros_like(dq_ref)
-    dk_ref[...] = jnp.zeros_like(dk_ref)
-    dv_ref[...] = jnp.zeros_like(dv_ref)
+    own = dot(x_ref[...], proj_ref[...]).astype(BF16)
+    own_ref[...] = own
+    half_temper = jnp.asarray(0.5 * temper, BF16)
+    scaled_ref[...] = own * half_temper
+    scaled_do_ref[...] = do_ref[...] * half_temper
 
     lane = iota((1, LANES), 1)
     group = LANES // head_size
@@ -251,84 +252,92 @@
     def spread(block):
         return jnp.concatenate([block * m for m in head_masks], axis=0)
 
-    def terms(scores_dot, grad_dot, allowed):
-        scores = scores_dot * temper
-        gates = 0.5 * jnp.tanh(0.5 * scores) + 0.5
-        scaled = gates * allowed
-        weights = (scores * scaled).astype(BF16)
-        slopes = scaled * (1.0 + scores * (1.0 - gates))
-        score_grad = (grad_dot * slopes * temper).astype(BF16)
+    def terms(half_scores, grad_dot, scale):
+        slant = jnp.tanh(half_scores)
+        gates = (1.0 + slant) * scale
+        weights = (half_scores * gates).astype(BF16)
+        score_grad = (grad_dot * (gates * (1.0 + half_scores * (1.0 - slant)))).astype(BF16)
         return weights, score_grad
 
-    row_ids = iota((tokens, span), 0)
-    lane_ids = iota((tokens, span), 1) % tokens
+    def put(ref, cols, value, first):
+        if first:
+            ref[:, cols] = value
+        else:
+            ref[:, cols] += value
+
+    def over_columns(begin, end):
+        held = begin(0)
+        for c in range(features // LANES):
+            after = begin(c + 1) if c + 1 < features // LANES else None
+            end(c, *held)
+            held = after
+
+    def lanes_at(offset, c):
+        return slice(offset + c * LANES, offset + (c + 1) * LANES)
+
+    def query_pass(source, offset, scale, first):
+        def begin(c):
+            keys = spread(source[:, lanes_at(offset, c)])
+            values = spread(source[:, lanes_at(offset + features, c)])
+            cols = lanes_at(0, c)
+            return keys, dot_nt(scaled_ref[:, cols], keys), dot_nt(scaled_do_ref[:, cols], values)
+
+        def end(c, keys, half_scores, grad_dot):
+            _, score_grad = terms(half_scores, grad_dot, scale)
+            put(dq_ref, lanes_at(0, c), dot(score_grad, keys), first)
+
+        over_columns(begin, end)
+
+    def key_pass(source, block, scale, first):
+        def begin(c):
+            cols = lanes_at(0, c)
+            queries = spread(source[:, cols])
+            grads = spread(do_all[block, :, cols])
+            return (
+                queries,
+                grads,
+                dot_nt(scaled_ref[:, lanes_at(features, c)], queries),
+                dot_nt(scaled_ref[:, lanes_at(2 * features, c)], grads),
+            )
+
+        def end(c, queries, grads, half_scores, grad_dot):
+            weights, score_grad = terms(half_scores, grad_dot, scale)
+            put(dk_ref, lanes_at(0, c), dot(score_grad, queries), first)
+            put(dv_ref, lanes_at(0, c), dot(weights, grads), first)
+
+        over_columns(begin, end)
 
     def visible(query_block, key_block):
-        seen = mask_ref[query_block, key_block] == 1
-        return jnp.where(seen | (query_block == key_block), history_scale, 0.0)
+        return jnp.where(mask_ref[query_block, key_block] == 1, history_scale, 0.0)
+
+    def own_block():
+        row_ids = iota((tokens, span), 0)
+        lane_ids = iota((tokens, span), 1) % tokens
+        query_pass(own_ref, features, jnp.where(lane_ids <= row_ids, history_scale, 0.0), True)
+        key_pass(own_ref, pos, jnp.where(row_ids <= lane_ids, history_scale, 0.0), True)
 
     def block_step(r):
         block = seq_peer(r)
-
         in_row, in_col = block // side == my_row, block % side == my_col
 
         @pl.when(jnp.logical_not(in_row | in_col))
         def _():
             x_relay(block, block).wait_recv()
 
-        @pl.when(block <= pos)
+        @pl.when(block < pos)
         def _():
-            @pl.when(block < pos)
-            def _():
-                other_ref[...] = dot(x_all[block], proj_ref[:, features:]).astype(BF16)
-
-            @pl.when(block == pos)
-            def _():
-                other_ref[...] = own_ref[:, features:]
-
-            allowed = jnp.where(
-                lane_ids <= row_ids + (pos - block) * tokens, visible(pos, block), 0.0
-            )
-            for c in range(features // LANES):
-                cols = slice(c * LANES, (c + 1) * LANES)
-                keys = spread(other_ref[:, cols])
-                values = spread(other_ref[:, features + c * LANES : features + (c + 1) * LANES])
-                _, score_grad = terms(
-                    dot_nt(own_ref[:, cols], keys), dot_nt(do_ref[:, cols], values), allowed
-                )
-                dq_ref[:, cols] += dot(score_grad, keys)
-
-        @pl.when(block >= pos)
+            other_ref[...] = dot(x_all[block], proj_ref[:, features:]).astype(BF16)
+            query_pass(other_ref, 0, visible(pos, block), False)
+
+        @pl.when(block > pos)
         def _():
-            @pl.when(block > pos)
-            def _():
-                other_ref[:, :features] = dot(x_all[block], proj_ref[:, :features]).astype(BF16)
-                to_seq(
-                    do_all.at[block], do_all.at[block], do_send.at[block], do_recv.at[block], block
-                ).wait_recv()
-
-            @pl.when(block == pos)
-            def _():
-                other_ref[:, :features] = own_ref[:, :features]
-
-            allowed = jnp.where(
-                row_ids <= lane_ids + (block - pos) * tokens, visible(block, pos), 0.0
-            )
-            for c in range(features // LANES):
-                cols = slice(c * LANES, (c + 1) * LANES)
-                queries = spread(other_ref[:, cols])
-                grads = spread(do_all[block, :, cols])
-                weights, score_grad = terms(
-                    dot_nt(own_ref[:, features + c * LANES : features + (c + 1) * LANES], queries),
-                    dot_nt(
-                        own_ref[:, 2 * features + c * LANES : 2 * features + (c + 1) * LANES], grads
-                    ),
-                    allowed,
-                )
-                dk_ref[:, cols] += dot(score_grad, queries)
-                dv_ref[:, cols] += dot(weights, grads)
-
-    block_step(0)
+            other_ref[:, :features] = dot(x_all[block], proj_ref[:, :features]).astype(BF16)
+            to_seq(
+                do_all.at[block], do_all.at[block], do_send.at[block], do_recv.at[block], block
+            ).wait_recv()
+            key_pass(other_ref, block, visible(block, pos), False)
+
+    own_block()
 
     def take_index(r):
         peer = table_peer(r)
@@ -610,6 +619,8 @@
             pltpu.VMEM((slab_rows, features), BF16),
             pltpu.VMEM((slab_rows, features), F32),
             pltpu.VMEM((tokens, 3 * features), BF16),
+            pltpu.VMEM((tokens, 3 * features), BF16),
+            pltpu.VMEM((tokens, features), BF16),
             pltpu.VMEM((tokens, 2 * features), BF16),
             pltpu.VMEM((tokens, features), F32),
             pltpu.VMEM((tokens, features), F32),

time: 48.7 us -> 47.8 us (0.982)
  Pallas kernels: 47.8 us -> 46.8 us
    pallas_call x1, Pallas kernels: 45.4 us -> 44.4 us  [body(): pl.pallas_call(functools.partial(kernel, seq_count, owner_count, capacity...]
where the time goes in v6:
time: 47.8 us; the launch traced here: 47.4 us
  Pallas kernels  46.8 us (98%)
  between operations  0.64 us (1%)
    pallas_call x1, Pallas kernels, body(): pl.pallas_call(functools.partial(kernel, seq_count, owner_count, capacity...  44.4 us
    pallas_call x1, Pallas kernels, body(): pl.pallas_call(pass_on, out_shape=tuple((jax.ShapeDtypeStruct(r.shape, r....  2.39 us

profile of v6, /device:TPU:0, one launch (start us, length us, event | category | flops | bytes accessed | tf_op | source)
XLA Modules:
  0.0 47.4 jit_solution(5148040156474777191)
XLA Ops:
  0.6 44.4 %shard_map.129 = (bf16[512,512]{1,0:T(8,128)(2,1)}, f32[512,512]{1,0:T(8,128)}, f32[4,128]{1,0:T(4,128)}, bf16[128,512]{1,0:T(8,128)(2,1)}) custom-call(bf16[128,512]{1,0:T(8,128)(2,1)} %bitcast.7, bf16[512,1536]{1,0:T(8,128)(2,1)} %proj_hbm.1, bf16[128,512]{1,0:T(8,128)(2,1)} %bitcast.8, s32[4,4]{1,0:T(4,128)} %mask_ref.1, s32[1,128]{1,0:T(1,128)} %ids_hbm.1, ...), custom_call_target="tpu_custom_call" | custom-call | tf_op jit(solution)/shard_map/pallas_call | solution.py:591
  45.0 2.4 %shard_map.130 = (bf16[512,512]{1,0:T(8,128)(2,1)}, f32[512,512]{1,0:T(8,128)}, f32[4,128]{1,0:T(4,128)}, bf16[128,512]{1,0:T(8,128)(2,1)}) custom-call(bf16[512,512]{1,0:T(8,128)(2,1)} %get-tuple-element.12.refs_0_, f32[512,512]{1,0:T(8,128)} %get-tuple-element.13.refs_1_, f32[4,128]{1,0:T(4,128)} %get-tuple-element.14.refs_2_, ...), custom_call_target="tpu_custom_call" | custom-call | tf_op jit(solution)/shard_map/pallas_call | solution.py:671

commit v7 on v6

--- a/solution.py
+++ b/solution.py
@@ -354,30 +354,6 @@
     each(1, seq_count, lambda r: idxf_copy(seq_peer(r)).start())
 
     each(1, side, relay_x)
-
-    slab_ids = iota((slab_rows, width), 0).astype(F32) + 1.0
-
-    def select(block):
-        select_ref[block] = jnp.where(
-            slab_ids == idx_all[block][0:1, :], 1.0, 0.0
-        ).astype(BF16)
-
-    select(pos)
-    slab_lanes = iota((LANES, slab_rows), 1).astype(F32) + 1.0
-    for c in range(width // LANES):
-        lanes = slice(c * LANES, (c + 1) * LANES)
-        replysel_ref[lanes, :] = jnp.where(
-            slab_lanes == to_col(idx_all[pos][0:1, lanes]), 1.0, 0.0
-        ).astype(BF16)
-
-    def select_other(r):
-        block = seq_peer(r)
-        to_seq(
-            idx_all.at[block], idx_all.at[block], idxf_ssem.at[block], idxf_rsem.at[block], block
-        ).wait_recv()
-        select(block)
-
-    each(1, seq_count, select_other)
     each(1, seq_count, block_step)
 
     stacked = jnp.concatenate(
@@ -456,6 +432,31 @@
 
     each(1, near, relay)
     pass_chunk(table_peer(near - 1))
+
+    slab_ids = iota((slab_rows, width), 0).astype(F32) + 1.0
+
+    def select(block):
+        select_ref[block] = jnp.where(
+            slab_ids == idx_all[block][0:1, :], 1.0, 0.0
+        ).astype(BF16)
+
+    select(pos)
+    slab_lanes = iota((LANES, slab_rows), 1).astype(F32) + 1.0
+    for c in range(width // LANES):
+        lanes = slice(c * LANES, (c + 1) * LANES)
+        replysel_ref[lanes, :] = jnp.where(
+            slab_lanes == to_col(idx_all[pos][0:1, lanes]), 1.0, 0.0
+        ).astype(BF16)
+
+    def select_other(r):
+        block = seq_peer(r)
+        to_seq(
+            idx_all.at[block], idx_all.at[block], idxf_ssem.at[block], idxf_rsem.at[block], block
+        ).wait_recv()
+        select(block)
+
+    each(1, seq_count, select_other)
+
     each(near, owner_count, lambda r: forward_far(take_chunk(r)))
 
     grad_ref[...] = dot(select_ref[pos], got[pos])
@@ -500,7 +501,7 @@
             rep_ssem.at[peer], rep_rsem.at[me], peer,
         )
 
-    each(1, owner_count, lambda r: reply_copy(table_peer(r)).start())
+    each(1, owner_count, lambda r: reply_copy(table_peer(owner_count - r)).start())
     stores = [
         pltpu.make_async_copy(nmom_ref, nmom_hbm, store_sem.at[0]),
         pltpu.make_async_copy(ntab_ref, ntab_hbm, store_sem.at[1]),

time: 47.8 us -> 47 us (0.983)
  Pallas kernels: 46.8 us -> 46.2 us
    pallas_call x1, Pallas kernels: 44.4 us -> 43.8 us  [body(): pl.pallas_call(functools.partial(kernel, seq_count, owner_count, capacity...]
where the time goes in v7:
time: 47 us; the launch traced here: 46.9 us
  Pallas kernels  46.2 us (98%)
  between operations  0.64 us (1%)
    pallas_call x1, Pallas kernels, body(): pl.pallas_call(functools.partial(kernel, seq_count, owner_count, capacity...  43.8 us
    pallas_call x1, Pallas kernels, body(): pl.pallas_call(pass_on, out_shape=tuple((jax.ShapeDtypeStruct(r.shape, r....  2.39 us

profile of v7, /device:TPU:0, one launch (start us, length us, event | category | flops | bytes accessed | tf_op | source)
XLA Modules:
  0.0 46.9 jit_solution(12965311108688963589)
XLA Ops:
  0.6 43.8 %shard_map.129 = (bf16[512,512]{1,0:T(8,128)(2,1)}, f32[512,512]{1,0:T(8,128)}, f32[4,128]{1,0:T(4,128)}, bf16[128,512]{1,0:T(8,128)(2,1)}) custom-call(bf16[128,512]{1,0:T(8,128)(2,1)} %bitcast.7, bf16[512,1536]{1,0:T(8,128)(2,1)} %proj_hbm.1, bf16[128,512]{1,0:T(8,128)(2,1)} %bitcast.8, s32[4,4]{1,0:T(4,128)} %mask_ref.1, s32[1,128]{1,0:T(1,128)} %ids_hbm.1, ...), custom_call_target="tpu_custom_call" | custom-call | tf_op jit(solution)/shard_map/pallas_call | solution.py:592
  44.5 2.4 %shard_map.130 = (bf16[512,512]{1,0:T(8,128)(2,1)}, f32[512,512]{1,0:T(8,128)}, f32[4,128]{1,0:T(4,128)}, bf16[128,512]{1,0:T(8,128)(2,1)}) custom-call(bf16[512,512]{1,0:T(8,128)(2,1)} %get-tuple-element.12.refs_0_, f32[512,512]{1,0:T(8,128)} %get-tuple-element.13.refs_1_, f32[4,128]{1,0:T(4,128)} %get-tuple-element.14.refs_2_, ...), custom_call_target="tpu_custom_call" | custom-call | tf_op jit(solution)/shard_map/pallas_call | solution.py:672

commit v8 on v7

--- a/solution.py
+++ b/solution.py
@@ -310,10 +310,14 @@
     def visible(query_block, key_block):
         return jnp.where(mask_ref[query_block, key_block] == 1, history_scale, 0.0)
 
-    def own_block():
+    def own_block(keys_too):
         row_ids = iota((tokens, span), 0)
         lane_ids = iota((tokens, span), 1) % tokens
-        query_pass(own_ref, features, jnp.where(lane_ids <= row_ids, history_scale, 0.0), True)
+        if not keys_too:
+            query_pass(
+                own_ref, features, jnp.where(lane_ids <= row_ids, history_scale, 0.0), True
+            )
+            return
         key_pass(own_ref, pos, jnp.where(row_ids <= lane_ids, history_scale, 0.0), True)
 
     def block_step(r):
@@ -337,7 +341,7 @@
             ).wait_recv()
             key_pass(other_ref, block, visible(block, pos), False)
 
-    own_block()
+    own_block(False)
 
     def take_index(r):
         peer = table_peer(r)
@@ -354,6 +358,7 @@
     each(1, seq_count, lambda r: idxf_copy(seq_peer(r)).start())
 
     each(1, side, relay_x)
+    own_block(True)
     each(1, seq_count, block_step)
 
     stacked = jnp.concatenate(

time: 47 us -> 47 us (level)
  no operation moved by 1% of the time
where the time goes in v8:
time: 47 us; the launch traced here: 46.9 us
  Pallas kernels  46.2 us (98%)
  between operations  0.64 us (1%)
    pallas_call x1, Pallas kernels, body(): pl.pallas_call(functools.partial(kernel, seq_count, owner_count, capacity...  43.8 us
    pallas_call x1, Pallas kernels, body(): pl.pallas_call(pass_on, out_shape=tuple((jax.ShapeDtypeStruct(r.shape, r....  2.39 us

profile of v8, /device:TPU:0, one launch (start us, length us, event | category | flops | bytes accessed | tf_op | source)
XLA Modules:
  0.0 46.9 jit_solution(12422680964650208454)
XLA Ops:
  0.6 43.8 %shard_map.129 = (bf16[512,512]{1,0:T(8,128)(2,1)}, f32[512,512]{1,0:T(8,128)}, f32[4,128]{1,0:T(4,128)}, bf16[128,512]{1,0:T(8,128)(2,1)}) custom-call(bf16[128,512]{1,0:T(8,128)(2,1)} %bitcast.7, bf16[512,1536]{1,0:T(8,128)(2,1)} %proj_hbm.1, bf16[128,512]{1,0:T(8,128)(2,1)} %bitcast.8, s32[4,4]{1,0:T(4,128)} %mask_ref.1, s32[1,128]{1,0:T(1,128)} %ids_hbm.1, ...), custom_call_target="tpu_custom_call" | custom-call | tf_op jit(solution)/shard_map/pallas_call | solution.py:597
  44.5 2.4 %shard_map.130 = (bf16[512,512]{1,0:T(8,128)(2,1)}, f32[512,512]{1,0:T(8,128)}, f32[4,128]{1,0:T(4,128)}, bf16[128,512]{1,0:T(8,128)(2,1)}) custom-call(bf16[512,512]{1,0:T(8,128)(2,1)} %get-tuple-element.12.refs_0_, f32[512,512]{1,0:T(8,128)} %get-tuple-element.13.refs_1_, f32[4,128]{1,0:T(4,128)} %get-tuple-element.14.refs_2_, ...), custom_call_target="tpu_custom_call" | custom-call | tf_op jit(solution)/shard_map/pallas_call | solution.py:677
